TPU v7x, 32 devices: a whole 2x2x4 slice. The times are simulated.
32 devices in a mesh: rep: 8 (over z, x), shard: 4 (over y, core).
Axes of the slice: x: 2, y: 2, z: 4, core: 2. Of those that a mesh axis runs over, the one named last changes fastest.
Arguments:
- tokens: bfloat16 [16384, 768], P(('rep', 'shard')), may hold values from -6 to 6
- cotangent: bfloat16 [16384, 768], P(('rep', 'shard')), may hold values from -6 to 6
- segment: int32 [16384], replicated, may hold values from 0 to 11, as said below
- w_qkv: bfloat16 [768, 2304], P('shard'), may hold values from -0.21875 to 0.21875
- bias_query: bfloat16 [768], P('shard'), may hold values from -1.5 to 1.5
- bias_value: bfloat16 [768], P('shard'), may hold values from -1.5 to 1.5
- w_out: bfloat16 [768, 768], P('shard'), may hold values from -6 to 6
- bias_out: bfloat16 [768], P('shard'), may hold values from -1.5 to 1.5
- ln1_gain: bfloat16 [768], P('shard'), may hold values from 0.5 to 1.5
- ln1_bias: bfloat16 [768], P('shard'), may hold values from -1.5 to 1.5
- ln2_gain: bfloat16 [768], P('shard'), may hold values from 0.5 to 1.5
- ln2_bias: bfloat16 [768], P('shard'), may hold values from -1.5 to 1.5
- w_up: bfloat16 [768, 3072], P('shard'), may hold values from -0.21875 to 0.21875
- bias_up: bfloat16 [3072], P('shard'), may hold values from -1.5 to 1.5
- w_down: bfloat16 [3072, 768], P('shard'), may hold values from -0.109375 to 0.109375
- bias_down: bfloat16 [768], P('shard'), may hold values from -1.5 to 1.5
Outputs:
- layer_out: float32 [16384, 768], P(('rep', 'shard'))
- grad_input: float32 [16384, 768], P(('rep', 'shard'))
- grad_w_qkv: float32 [768, 2304], P('shard')
- grad_bias_query: float32 [768], P('shard')
- grad_bias_value: float32 [768], P('shard')
- grad_w_out: float32 [768, 768], P('shard')
- grad_bias_out: float32 [768], P('shard')
- grad_ln1_gain: float32 [768], P('shard')
- grad_ln1_bias: float32 [768], P('shard')
- grad_ln2_gain: float32 [768], P('shard')
- grad_ln2_bias: float32 [768], P('shard')
- grad_w_up: float32 [768, 3072], P('shard')
- grad_bias_up: float32 [3072], P('shard')
- grad_w_down: float32 [3072, 768], P('shard')
- grad_bias_down: float32 [768], P('shard')
Inputs may be any that keep to these rules, and one draw needn't show every extreme that they name: `segment`: never falls along the stream and starts at 0; each run of one value is one sequence of 1024 to 2048 tokens, one run holds exactly 2048; every aligned stretch of 4096 tokens holds exactly three whole sequences.
All inputs are finite; a program needn't handle non-finite values.
Results may differ from a plain program's by a relative error of at most 0.013.
Values may be sent and summed in bfloat16 or wider, within the bound.
A program may use at most 320 MiB of HBM per device.

v0:
```python
import jax
import jax.numpy as jnp
from jax import lax
from jax.sharding import PartitionSpec as P

H = 12
LOOK = 4


norm_eps = 1e-05
masked_value = -1e30


def from_behind(value, axis, steps):
    count = lax.axis_size(axis)
    first, last = (max(0, -steps), min(count, count - steps))
    return lax.ppermute(value, axis, [(source, source + steps) for source in range(first, last)])


def layer_norm(values, gain, offset):
    centre = jnp.mean(values, axis=-1, keepdims=True)
    centred = values - centre
    variance = jnp.mean(centred * centred, axis=-1, keepdims=True)
    return centred * lax.rsqrt(variance + norm_eps) * gain + offset


def gelu_tanh(values):
    return jax.nn.gelu(values, approximate=True)


def matmul(left, right):
    return jnp.dot(left, right, preferred_element_type=jnp.float32)


def left_times(left, right):
    return lax.dot_general(
        left, right, (((0,), (0,)), ((), ())), preferred_element_type=jnp.float32
    )


def right_times(left, right):
    return lax.dot_general(
        left, right, (((1,), (1,)), ((), ())), preferred_element_type=jnp.float32
    )


def column_sum(values):
    return jnp.sum(values.astype(jnp.float32), axis=0)


def body(
    tokens,
    cotangent,
    segment,
    w_qkv,
    bias_query,
    bias_value,
    w_out,
    bias_out,
    ln1_gain,
    ln1_bias,
    ln2_gain,
    ln2_bias,
    w_up,
    bias_up,
    w_down,
    bias_down,
):
    gathered = (
        lax.all_gather(w_qkv, "shard", axis=0, tiled=True),
        lax.all_gather(bias_query, "shard", axis=0, tiled=True),
        lax.all_gather(bias_value, "shard", axis=0, tiled=True),
        lax.all_gather(w_out, "shard", axis=0, tiled=True),
        lax.all_gather(bias_out, "shard", axis=0, tiled=True),
        lax.all_gather(ln1_gain, "shard", axis=0, tiled=True),
        lax.all_gather(ln1_bias, "shard", axis=0, tiled=True),
        lax.all_gather(ln2_gain, "shard", axis=0, tiled=True),
        lax.all_gather(ln2_bias, "shard", axis=0, tiled=True),
        lax.all_gather(w_up, "shard", axis=0, tiled=True),
        lax.all_gather(bias_up, "shard", axis=0, tiled=True),
        lax.all_gather(w_down, "shard", axis=0, tiled=True),
        lax.all_gather(bias_down, "shard", axis=0, tiled=True),
    )
    (
        full_qkv,
        query_bias,
        value_bias,
        full_wout,
        out_bias,
        gain_one,
        offset_one,
        gain_two,
        offset_two,
        full_wup,
        up_bias,
        full_wdown,
        down_bias,
    ) = gathered
    tok_rows, width = tokens.shape
    head_size = width // H
    score_scale = head_size ** (-0.5)
    position = lax.axis_index(("rep", "shard"))
    local_pos = jnp.arange(tok_rows, dtype=jnp.int32)
    query_pos = position * tok_rows + local_pos
    query_seg = lax.dynamic_slice_in_dim(segment, position * tok_rows, tok_rows, 0)
    allowed = []
    for distance in range(LOOK + 1):
        source = position - distance
        key_seg = lax.dynamic_slice_in_dim(segment, jnp.maximum(source, 0) * tok_rows, tok_rows, 0)
        key_pos = source * tok_rows + local_pos
        visible = (
            (query_seg[:, None] == key_seg[None, :])
            & (key_pos[None, :] <= query_pos[:, None])
            & (key_pos[None, :] >= 0)
        )
        allowed.append(visible[None])
    inputs = tokens.astype(jnp.float32)
    normed, norm_one_back = jax.vjp(
        layer_norm, inputs, gain_one.astype(jnp.float32), offset_one.astype(jnp.float32)
    )
    normed_low = normed.astype(jnp.bfloat16)
    joined_bias = jnp.concatenate([query_bias, jnp.zeros_like(query_bias), value_bias]).astype(
        jnp.float32
    )
    projected = (matmul(normed_low, full_qkv) + joined_bias).astype(jnp.bfloat16)
    queries = projected[:, :width].reshape(tok_rows, H, head_size)
    own_pairs = projected[:, width:]
    kv_pieces = [own_pairs]
    for distance in range(1, LOOK + 1):
        kv_pieces.append(from_behind(own_pairs, ("rep", "shard"), distance))
    key_list = [piece[:, :width].reshape(tok_rows, H, head_size) for piece in kv_pieces]
    value_list = [piece[:, width:].reshape(tok_rows, H, head_size) for piece in kv_pieces]

    def piece_scores(distance):
        raw = jnp.einsum(
            "qhd,khd->hqk", queries, key_list[distance], preferred_element_type=jnp.float32
        )
        return raw * score_scale

    running_max = jnp.full((H, tok_rows, 1), masked_value, jnp.float32)
    running_sum = jnp.zeros((H, tok_rows, 1), jnp.float32)
    for distance in range(LOOK + 1):
        scores = jnp.where(allowed[distance], piece_scores(distance), masked_value)
        new_max = jnp.maximum(running_max, jnp.max(scores, axis=-1, keepdims=True))
        fresh = jnp.sum(
            jnp.where(allowed[distance], jnp.exp(scores - new_max), 0.0), axis=-1, keepdims=True
        )
        running_sum = running_sum * jnp.exp(running_max - new_max) + fresh
        running_max = new_max
    totals = running_max + jnp.log(running_sum)

    def piece_weights(distance):
        return jnp.where(allowed[distance], jnp.exp(piece_scores(distance) - totals), 0.0)

    mixed = jnp.zeros((tok_rows, H, head_size), jnp.float32)
    for distance in range(LOOK + 1):
        weights_low = piece_weights(distance).astype(jnp.bfloat16)
        mixed = mixed + jnp.einsum(
            "hqk,khd->qhd", weights_low, value_list[distance], preferred_element_type=jnp.float32
        )
    mixed_low = mixed.reshape(tok_rows, width).astype(jnp.bfloat16)
    middle = inputs + matmul(mixed_low, full_wout) + out_bias.astype(jnp.float32)
    second, norm_two_back = jax.vjp(
        layer_norm, middle, gain_two.astype(jnp.float32), offset_two.astype(jnp.float32)
    )
    second_low = second.astype(jnp.bfloat16)
    hidden = matmul(second_low, full_wup) + up_bias.astype(jnp.float32)
    active, gelu_back = jax.vjp(gelu_tanh, hidden)
    active_low = active.astype(jnp.bfloat16)
    layer_out = middle + matmul(active_low, full_wdown) + down_bias.astype(jnp.float32)
    grad_out = cotangent.astype(jnp.float32)
    grad_wdown = left_times(active_low, cotangent)
    grad_down_bias = jnp.sum(grad_out, axis=0)
    grad_active = right_times(cotangent, full_wdown)
    (grad_hidden,) = gelu_back(grad_active)
    hidden_low = grad_hidden.astype(jnp.bfloat16)
    grad_wup = left_times(second_low, hidden_low)
    grad_up_bias = column_sum(hidden_low)
    grad_second = right_times(hidden_low, full_wup)
    grad_middle_norm, grad_gain_two, grad_offset_two = norm_two_back(grad_second)
    grad_middle = grad_out + grad_middle_norm
    middle_low = grad_middle.astype(jnp.bfloat16)
    grad_wout = left_times(mixed_low, middle_low)
    grad_out_bias = column_sum(middle_low)
    grad_mixed = (
        right_times(middle_low, full_wout).astype(jnp.bfloat16).reshape(tok_rows, H, head_size)
    )

    def piece_slopes(distance):
        return jnp.einsum(
            "qhd,khd->hqk", grad_mixed, value_list[distance], preferred_element_type=jnp.float32
        )

    row_dots = jnp.zeros((H, tok_rows, 1), jnp.float32)
    for distance in range(LOOK + 1):
        row_dots = row_dots + jnp.sum(
            piece_slopes(distance) * piece_weights(distance), axis=-1, keepdims=True
        )
    grad_queries = jnp.zeros((tok_rows, H, head_size), jnp.float32)
    grad_pieces = []
    for distance in range(LOOK + 1):
        weights = piece_weights(distance)
        grad_scores = (weights * (piece_slopes(distance) - row_dots)).astype(jnp.bfloat16)
        grad_queries = grad_queries + jnp.einsum(
            "hqk,khd->qhd", grad_scores, key_list[distance], preferred_element_type=jnp.float32
        )
        grad_keys = (
            jnp.einsum("hqk,qhd->khd", grad_scores, queries, preferred_element_type=jnp.float32)
            * score_scale
        )
        grad_values = jnp.einsum(
            "hqk,qhd->khd",
            weights.astype(jnp.bfloat16),
            grad_mixed,
            preferred_element_type=jnp.float32,
        )
        grad_pieces.append(
            jnp.concatenate(
                [grad_keys.reshape(tok_rows, width), grad_values.reshape(tok_rows, width)], axis=1
            )
        )
    grad_pairs = grad_pieces[0]
    for distance in range(1, LOOK + 1):
        grad_pairs = grad_pairs + from_behind(
            grad_pieces[distance].astype(jnp.bfloat16), ("rep", "shard"), -distance
        ).astype(jnp.float32)
    grad_projected = jnp.concatenate(
        [(grad_queries * score_scale).reshape(tok_rows, width), grad_pairs], axis=1
    ).astype(jnp.bfloat16)
    grad_wqkv = left_times(normed_low, grad_projected)
    bias_grads = column_sum(grad_projected)
    grad_query_bias = bias_grads[:width]
    grad_value_bias = bias_grads[2 * width :]
    grad_normed = right_times(grad_projected, full_qkv)
    grad_input_norm, grad_gain_one, grad_offset_one = norm_one_back(grad_normed)
    grad_input = grad_middle + grad_input_norm
    local_grads = (
        grad_wqkv,
        grad_query_bias,
        grad_value_bias,
        grad_wout,
        grad_out_bias,
        grad_gain_one,
        grad_offset_one,
        grad_gain_two,
        grad_offset_two,
        grad_wup,
        grad_up_bias,
        grad_wdown,
        grad_down_bias,
    )
    shards = (
        lax.psum_scatter(
            local_grads[0].astype(jnp.bfloat16), "shard", scatter_dimension=0, tiled=True
        ).astype(jnp.float32),
        lax.psum_scatter(
            local_grads[1].astype(jnp.bfloat16), "shard", scatter_dimension=0, tiled=True
        ).astype(jnp.float32),
        lax.psum_scatter(
            local_grads[2].astype(jnp.bfloat16), "shard", scatter_dimension=0, tiled=True
        ).astype(jnp.float32),
        lax.psum_scatter(
            local_grads[3].astype(jnp.bfloat16), "shard", scatter_dimension=0, tiled=True
        ).astype(jnp.float32),
        lax.psum_scatter(
            local_grads[4].astype(jnp.bfloat16), "shard", scatter_dimension=0, tiled=True
        ).astype(jnp.float32),
        lax.psum_scatter(
            local_grads[5].astype(jnp.bfloat16), "shard", scatter_dimension=0, tiled=True
        ).astype(jnp.float32),
        lax.psum_scatter(
            local_grads[6].astype(jnp.bfloat16), "shard", scatter_dimension=0, tiled=True
        ).astype(jnp.float32),
        lax.psum_scatter(
            local_grads[7].astype(jnp.bfloat16), "shard", scatter_dimension=0, tiled=True
        ).astype(jnp.float32),
        lax.psum_scatter(
            local_grads[8].astype(jnp.bfloat16), "shard", scatter_dimension=0, tiled=True
        ).astype(jnp.float32),
        lax.psum_scatter(
            local_grads[9].astype(jnp.bfloat16), "shard", scatter_dimension=0, tiled=True
        ).astype(jnp.float32),
        lax.psum_scatter(
            local_grads[10].astype(jnp.bfloat16), "shard", scatter_dimension=0, tiled=True
        ).astype(jnp.float32),
        lax.psum_scatter(
            local_grads[11].astype(jnp.bfloat16), "shard", scatter_dimension=0, tiled=True
        ).astype(jnp.float32),
        lax.psum_scatter(
            local_grads[12].astype(jnp.bfloat16), "shard", scatter_dimension=0, tiled=True
        ).astype(jnp.float32),
    )
    summed = lax.psum(
        (
            shards[0],
            shards[1],
            shards[2],
            shards[3],
            shards[4],
            shards[5],
            shards[6],
            shards[7],
            shards[8],
            shards[9],
            shards[10],
            shards[11],
            shards[12],
        ),
        "rep",
    )
    return (
        layer_out,
        grad_input,
        summed[0],
        summed[1],
        summed[2],
        summed[3],
        summed[4],
        summed[5],
        summed[6],
        summed[7],
        summed[8],
        summed[9],
        summed[10],
        summed[11],
        summed[12],
    )


def solution(mesh):
    placed = (
        P(("rep", "shard"), None),
        P(("rep", "shard"), None),
        P(),
        P("shard", None),
        P("shard"),
        P("shard"),
        P("shard", None),
        P("shard"),
        P("shard"),
        P("shard"),
        P("shard"),
        P("shard"),
        P("shard", None),
        P("shard"),
        P("shard", None),
        P("shard"),
    )
    return jax.shard_map(
        body,
        mesh=mesh,
        in_specs=placed,
        out_specs=(
            P(("rep", "shard"), None),
            P(("rep", "shard"), None),
            P("shard", None),
            P("shard"),
            P("shard"),
            P("shard", None),
            P("shard"),
            P("shard"),
            P("shard"),
            P("shard"),
            P("shard"),
            P("shard", None),
            P("shard"),
            P("shard", None),
            P("shard"),
        ),
        check_vma=False,
    )
```

profile of v0, /device:TPU:0, one launch (start us, length us, event | category | flops | bytes accessed | tf_op | source)
XLA Modules:
  0.0 1021.1 jit_solution(9077269757035026077)
XLA Ops:
  18.0 13.5 %all-reduce.19 = (bf16[768]{0:T(1024)(128)(2,1)S(1)}, bf16[768]{0:T(1024)(128)(2,1)S(1)}, bf16[768]{0:T(1024)(128)(2,1)S(1)}, bf16[768]{0:T(1024)(128)(2,1)S(1)}...) all-reduce(bf16[768]{0:T(1024)(128)(2,1)S(1)} %dynamic-update-slice, ...), channel_id=1, replica_groups=mesh['rep'=8,'shard'=4] {'shard'}, use_global_device_ids=true, to_apply=%add.3 | all-reduce | flops 5376 | bytes 21504
  34.4 9.0 all-gather.6.cloned.1.call-done
  43.4 4.4 fusion.12
  50.5 4.6 collective-permute-start.3
  56.1 3.6 collective-permute-start.1
  66.1 45.5 %all-gather = bf16[4,1,768]{2,1,0:T(2,128)(2,1)S(1)} all-gather(bf16[1,1,768]{2,1,0:T(2,128)(2,1)S(1)} %reshape.751), channel_id=1, replica_groups=mesh['rep'=8,'shard'=4] {'shard'}, dimensions={0}, use_global_device_ids=true | all-gather | bytes 7680 | tf_op jit(solution)/shard_map/all_gather | solution.py:80
  111.6 29.4 %collective-permute-start.2 = (bf16[512,1536]{1,0:T(8,128)(2,1)}, bf16[512,1536]{1,0:T(8,128)(2,1)}, u32[]{:S(2)}, u32[]{:S(2)}) collective-permute-start(bf16[512,1536]{1,0:T(8,128)(2,1)} %slice.63), channel_id=1, source_target_pairs={{0,3},{1,4},{2,5},{3,6},{4,7},{5,8},{6,9},{7,10},{8,11},{9,12},{10... | collective-permute-start | bytes 4718600 | tf_op jit(solution)/shard_map/ppermute | solution.py:17
  146.9 6.6 select_reduce_fusion.9
  166.9 3.5 select_reduce_fusion.5
  172.6 7.3 select_reduce_fusion.8
  179.9 7.0 select_reduce_fusion.6
  188.2 9.2 select_reduce_fusion.2
  197.5 10.1 select_reduce_fusion
  207.7 3.8 select_reduce_fusion.4
  217.6 8.4 fusion.44
  226.0 8.4 fusion.48
  234.4 3.9 fusion.41
  238.3 6.0 fusion.38
  252.2 8.2 fusion.78
  260.4 9.9 fusion.80
  270.4 3.5 multiply_reduce_fusion.5
  279.8 6.4 fusion.97
  286.2 6.4 fusion.98
  292.6 7.0 fusion.99
  299.7 6.4 fusion.96
  309.4 41.9 %multiply_reduce_fusion.3 = (f32[12,512]{1,0:T(8,128)S(1)}, f32[12,512]{1,0:T(8,128)S(1)}, f32[12,512]{1,0:T(8,128)S(1)}, f32[12,512]{1,0:T(8,128)S(1)}, f32[12,512]{1,0:T(8,128)S(1)}, /*index=5*/f32[12,512,512]{1,2,0:T(8,128)}) fusion(f32[12,512,512]{1,2,0:T(8,128)} %get-tuple-element.107, f32[12,512]{1,0:T(8,128)S(1)} %log_add_fusion, ...), kind=kOutput, calls=%fused_computation.8 | convolution fusion | flops 481265664 | bytes 128860160 | tf_op jit(solution)/shard_map/qhd,khd->hqk/dot_general | solution.py:190
  351.3 51.1 %multiply_convert_fusion.3 = (bf16[12,512,512]{1,2,0:T(8,128)(2,1)}, bf16[12,512,512]{1,2,0:T(8,128)(2,1)}, bf16[12,512,512]{1,2,0:T(8,128)(2,1)}, bf16[12,512,512]{1,2,0:T(8,128)(2,1)}, bf16[12,512,512]{1,2,0:T(8,128)(2,1)}) fusion(f32[12,512,512]{1,2,0:T(8,128)} %get-tuple-element.113, f32[12,512,512]{1,2,0:T(8,128)} %get-tuple-element.107, ...), kind=kLoop, calls=%fused_computation.3 | loop fusion | flops 94371840 | bytes 158646272 | tf_op jit(solution)/shard_map/convert_element_type | solution.py:203
  402.5 4.4 fusion.101
  410.5 7.1 convolution_convert_fusion.7
  422.9 3.7 convolution_convert_fusion.6
  426.6 5.3 fusion.103
  431.9 5.7 multiply_convert_fusion.8
  442.8 5.5 fusion.100
  461.0 5.7 multiply_convert_fusion.6
  466.7 5.2 convolution_multiply_fusion
  474.5 57.0 %collective-permute-done.5 = bf16[512,1536]{0,1:T(8,128)(2,1)} collective-permute-done((bf16[512,1536]{0,1:T(8,128)(2,1)}, bf16[512,1536]{0,1:T(8,128)(2,1)}, u32[]{:S(2)}, u32[]{:S(2)}) %collective-permute-start.5) | collective-permute-done | bytes 1572896 | tf_op jit(solution)/shard_map/ppermute | solution.py:17
  531.5 4.4 collective-permute-done.6
  535.9 47.1 %collective-permute-done.7 = bf16[512,1536]{0,1:T(8,128)(2,1)} collective-permute-done((bf16[512,1536]{0,1:T(8,128)(2,1)}, bf16[512,1536]{0,1:T(8,128)(2,1)}, u32[]{:S(2)}, u32[]{:S(2)}) %collective-permute-start.7) | collective-permute-done | bytes 1572896 | tf_op jit(solution)/shard_map/ppermute | solution.py:17
  583.0 3.9 fusion.16
  588.1 4.1 convolution_convert_fusion.2
  592.4 6.5 convolution_convert_fusion.1
  599.2 9.7 convolution_convert_fusion
  612.3 5.1 fusion.79
  619.5 11.5 %all-reduce.18 = (bf16[768]{0:T(1024)(128)(2,1)S(1)}, bf16[768]{0:T(1024)(128)(2,1)S(1)}, bf16[768]{0:T(1024)(128)(2,1)S(1)}, bf16[768]{0:T(1024)(128)(2,1)S(1)}...) all-reduce(bf16[768]{0:T(1024)(128)(2,1)S(1)} %dynamic-update-slice, ...), channel_id=1, replica_groups=mesh['rep'=8,'shard'=4] {'shard'}, use_global_device_ids=true, to_apply=%add.7 | all-reduce | flops 9984 | bytes 39936
  635.0 9.3 add_add_fusion.4
  644.2 40.2 %reduce-scatter.9.cloned.1.call-done = bf16[192,3072]{1,0:T(8,128)(2,1)} async-done(((bf16[768,3072]{1,0:T(8,128)(2,1)}), bf16[192,3072]{1,0:T(8,128)(2,1)}) %reduce-scatter.9.cloned.1.call-update) | async-done | bytes 1179664 | tf_op jit(solution)/shard_map/reduce_scatter | solution.py:280
  684.4 50.6 %reduce-scatter.11.cloned.1.call-done = bf16[768,768]{1,0:T(8,128)(2,1)} async-done(((bf16[3072,768]{1,0:T(8,128)(2,1)}), bf16[768,768]{1,0:T(8,128)(2,1)}) %reduce-scatter.11.cloned.1.call-update) | async-done | bytes 1179664 | tf_op jit(solution)/shard_map/reduce_scatter | solution.py:286
  735.0 279.1 %all-reduce.21 = (f32[192,2304]{1,0:T(8,128)}, f32[192]{0:T(256)}, f32[192]{0:T(256)}, f32[192,768]{1,0:T(8,128)}, f32[192]{0:T(256)}, /*index=5*/f32[192]{0:T(2...) all-reduce(bf16[192,2304]{1,0:T(8,128)(2,1)} %reduce-scatter.5.clon, ...), channel_id=1, replica_groups=mesh['rep'=8,'shard'=4] {'rep'}, use_global_device_ids=true, to_apply=%region_24.25 | all-reduce | flops 1771776 | bytes 10635264 | tf_op jit(solution)/shard_map/psum | solution.py:293
  (384 shorter events, 107.1 us)
Async XLA Ops:
  7.2 36.2 %all-gather.6.cloned.1.call-start = ((), (), s32[]{:S(2)}) async-start(), calls=%async_computation.4 | async-start | bytes 4423680 | tf_op jit(solution)/shard_map/all_gather | solution.py:70
  7.9 240.3 %all-gather.8.cloned.1.call-start = ((), (), s32[]{:S(2)}) async-start(), calls=%async_computation.5 | async-start | bytes 1474560 | tf_op jit(solution)/shard_map/all_gather | solution.py:73
  8.7 243.5 %all-gather.10.cloned.1.call-start = ((), (), s32[]{:S(2)}) async-start(), calls=%async_computation.6 | async-start | bytes 5898240 | tf_op jit(solution)/shard_map/all_gather | solution.py:79
  9.4 251.0 %all-gather.12.cloned.1.call-start = ((), (), s32[]{:S(2)}) async-start(), calls=%async_computation.7 | async-start | bytes 5898240 | tf_op jit(solution)/shard_map/all_gather | solution.py:81
  10.0 634.3 %reduce-scatter.7.cloned.1.call-start = ((), (), s32[]{:S(2)}) async-start(), calls=%async_computation.9 | async-start | bytes 1474560 | tf_op jit(solution)/shard_map/reduce_scatter | solution.py:262
  31.5 16.3 %copy-start.63 = (f32[768]{0:T(1024)}, f32[768]{0:T(1024)S(1)}, u32[]{:S(2)}) copy-start(f32[768]{0:T(1024)S(1)} %convert_element_type.185) | copy-start | bytes 9220
  31.5 16.3 %copy-start.84 = (f32[768]{0:T(1024)}, f32[768]{0:T(1024)S(1)}, u32[]{:S(2)}) copy-start(f32[768]{0:T(1024)S(1)} %convert_element_type.186) | copy-start | bytes 9220
  32.8 15.0 %copy-start.65 = (f32[512]{0:T(512)}, f32[512]{0:T(512)S(1)}, u32[]{:S(2)}) copy-start(f32[512]{0:T(512)S(1)} %broadcast_multiply_fusion.1) | copy-start | bytes 6148
  34.4 13.5 %copy-start.73 = (f32[512]{0:T(512)}, f32[512]{0:T(512)S(1)}, u32[]{:S(2)}) copy-start(f32[512]{0:T(512)S(1)} %fusion.26) | copy-start | bytes 6148
  34.4 13.5 %copy-start.67 = (f32[512]{0:T(512)}, f32[512]{0:T(512)S(1)}, u32[]{:S(2)}) copy-start(f32[512]{0:T(512)S(1)} %fusion.50) | copy-start | bytes 6148
  34.4 31.7 %copy-start.91 = (bf16[768]{0:T(1024)(128)(2,1)S(1)}, bf16[768]{0:T(1024)(128)(2,1)}, u32[]{:S(2)}) copy-start(bf16[768]{0:T(1024)(128)(2,1)} %param.29) | copy-start | bytes 4612
  50.5 103.0 %collective-permute-start.3 = (bf16[512,1536]{1,0:T(8,128)(2,1)}, bf16[512,1536]{1,0:T(8,128)(2,1)}, u32[]{:S(2)}, u32[]{:S(2)}) collective-permute-start(bf16[512,1536]{1,0:T(8,128)(2,1)} %slice.63), channel_id=1, source_target_pairs={{0,4},{1,5},{2,6},{3,7},{4,8},{5,9},{6,10},{7,11},{8,12},{9,13},{1... | collective-permute-start | bytes 4718600 | tf_op jit(solution)/shard_map/ppermute | solution.py:17
  56.1 100.9 %collective-permute-start.1 = (bf16[512,1536]{1,0:T(8,128)(2,1)}, bf16[512,1536]{1,0:T(8,128)(2,1)}, u32[]{:S(2)}, u32[]{:S(2)}) collective-permute-start(bf16[512,1536]{1,0:T(8,128)(2,1)} %slice.63), channel_id=1, source_target_pairs={{0,2},{1,3},{2,4},{3,5},{4,6},{5,7},{6,8},{7,9},{8,10},{9,11},{10,... | collective-permute-start | bytes 4718600 | tf_op jit(solution)/shard_map/ppermute | solution.py:17
  59.7 100.0 %collective-permute-start = (bf16[512,1536]{1,0:T(8,128)(2,1)}, bf16[512,1536]{1,0:T(8,128)(2,1)}, u32[]{:S(2)}, u32[]{:S(2)}) collective-permute-start(bf16[512,1536]{1,0:T(8,128)(2,1)} %slice.63), channel_id=1, source_target_pairs={{0,1},{1,2},{2,3},{3,4},{4,5},{5,6},{6,7},{7,8},{8,9},{9,10},{10,1... | collective-permute-start | bytes 4718600 | tf_op jit(solution)/shard_map/ppermute | solution.py:17
  64.9 88.6 %copy-start.23 = (pred[512,512]{0,1:T(8,128)(4,1)}, pred[512,512]{0,1:T(8,128)(4,1)S(1)}, u32[]{:S(2)}) copy-start(pred[512,512]{0,1:T(8,128)(4,1)S(1)} %get-tuple-element.93) | copy-start | bytes 786436
  65.5 208.4 %copy-start.75 = (f32[768]{0:T(1024)}, f32[768]{0:T(1024)S(1)}, u32[]{:S(2)}) copy-start(f32[768]{0:T(1024)S(1)} %convert_element_type.197) | copy-start | bytes 9220
  111.6 148.8 %copy-start.77 = (f32[4,1,768]{2,1,0:T(1,128)}, f32[4,1,768]{2,1,0:T(1,128)S(1)}, u32[]{:S(2)}) copy-start(f32[4,1,768]{2,1,0:T(1,128)S(1)} %convert_element_type.238) | copy-start | bytes 36868
  111.6 51.0 %collective-permute-start.2 = (bf16[512,1536]{1,0:T(8,128)(2,1)}, bf16[512,1536]{1,0:T(8,128)(2,1)}, u32[]{:S(2)}, u32[]{:S(2)}) collective-permute-start(bf16[512,1536]{1,0:T(8,128)(2,1)} %slice.63), channel_id=1, source_target_pairs={{0,3},{1,4},{2,5},{3,6},{4,7},{5,8},{6,9},{7,10},{8,11},{9,12},{10... | collective-permute-start | bytes 4718600 | tf_op jit(solution)/shard_map/ppermute | solution.py:17
  144.0 35.9 %copy-start.2 = (bf16[512,768]{0,1:T(8,128)(2,1)}, bf16[512,768]{0,1:T(8,128)(2,1)S(1)}, u32[]{:S(2)}) copy-start(bf16[512,768]{0,1:T(8,128)(2,1)S(1)} %copy.124) | copy-start | bytes 2359300
  166.9 13.0 %copy-start.12 = (bf16[512,768]{0,1:T(8,128)(2,1)}, bf16[512,768]{0,1:T(8,128)(2,1)S(1)}, u32[]{:S(2)}) copy-start(bf16[512,768]{0,1:T(8,128)(2,1)S(1)} %copy.128) | copy-start | bytes 2359300
  170.4 27.0 %copy-start = (f32[12,512,512]{1,2,0:T(8,128)}, f32[12,512,512]{1,2,0:T(8,128)S(1)}, u32[]{:S(2)}) copy-start(f32[12,512,512]{1,2,0:T(8,128)S(1)} %get-tuple-element.101) | copy-start | bytes 37748740
  172.6 15.7 %copy-start.1 = (f32[12,512,512]{1,2,0:T(8,128)}, f32[12,512,512]{1,2,0:T(8,128)S(1)}, u32[]{:S(2)}) copy-start(f32[12,512,512]{1,2,0:T(8,128)S(1)} %get-tuple-element.105) | copy-start | bytes 37748740
  211.7 14.2 %copy-start.34 = (bf16[512,768]{0,1:T(8,128)(2,1)}, bf16[512,768]{0,1:T(8,128)(2,1)S(1)}, u32[]{:S(2)}) copy-start(bf16[512,768]{0,1:T(8,128)(2,1)S(1)} %copy.131) | copy-start | bytes 2359300
  217.5 16.8 %slice-start.12 = ((s8[12582912]{0:T(1024)(128)(4,1)}), s8[4194304]{0:T(1024)(128)(4,1)S(1)}, s32[]{:S(2)}) async-start(s8[12582912]{0:T(1024)(128)(4,1)} %bitcast.125), calls=%async_computation.24 | async-start | bytes 8388608
  217.6 16.8 %slice-start.13 = ((s8[12582912]{0:T(1024)(128)(4,1)}), s8[4194304]{0:T(1024)(128)(4,1)S(1)}, s32[]{:S(2)}) async-start(s8[12582912]{0:T(1024)(128)(4,1)} %bitcast.125), calls=%async_computation.25 | async-start | bytes 8388608
  250.7 23.2 %copy-start.71 = (f32[512]{0:T(512)}, f32[512]{0:T(512)S(1)}, u32[]{:S(2)}) copy-start(f32[512]{0:T(512)S(1)} %broadcast_multiply_fusion) | copy-start | bytes 6148
  252.1 21.8 %copy-start.79 = (f32[512]{0:T(512)}, f32[512]{0:T(512)S(1)}, u32[]{:S(2)}) copy-start(f32[512]{0:T(512)S(1)} %fusion.51) | copy-start | bytes 6148
  292.6 13.4 %slice-start.18 = ((s8[12582912]{0:T(1024)(128)(4,1)}), s8[4194304]{0:T(1024)(128)(4,1)S(1)}, s32[]{:S(2)}) async-start(s8[12582912]{0:T(1024)(128)(4,1)} %bitcast.129), calls=%async_computation.30 | async-start | bytes 8388608
  292.6 13.4 %slice-start.19 = ((s8[12582912]{0:T(1024)(128)(4,1)}), s8[4194304]{0:T(1024)(128)(4,1)S(1)}, s32[]{:S(2)}) async-start(s8[12582912]{0:T(1024)(128)(4,1)} %bitcast.129), calls=%async_computation.31 | async-start | bytes 8388608
  422.9 14.7 %slice-start.3 = ((s8[12582912]{0:T(1024)(128)(4,1)}), s8[4194304]{0:T(1024)(128)(4,1)S(1)}, s32[]{:S(2)}) async-start(s8[12582912]{0:T(1024)(128)(4,1)} %bitcast.119), calls=%async_computation.15 | async-start | bytes 8388608
  422.9 14.7 %slice-start.4 = ((s8[12582912]{0:T(1024)(128)(4,1)}), s8[4194304]{0:T(1024)(128)(4,1)S(1)}, s32[]{:S(2)}) async-start(s8[12582912]{0:T(1024)(128)(4,1)} %bitcast.119), calls=%async_computation.16 | async-start | bytes 8388608
  442.8 13.4 %slice-start.23 = ((s8[6291456]{0:T(1024)(128)(4,1)}), s8[4194304]{0:T(1024)(128)(4,1)S(1)}, s32[]{:S(2)}) async-start(s8[6291456]{0:T(1024)(128)(4,1)} %bitcast.143), calls=%async_computation.35 | async-start | bytes 8388608
  442.8 13.4 %slice-start.24 = ((s8[6291456]{0:T(1024)(128)(4,1)}), s8[2097152]{0:T(1024)(128)(4,1)S(1)}, s32[]{:S(2)}) async-start(s8[6291456]{0:T(1024)(128)(4,1)} %bitcast.143), calls=%async_computation.36 | async-start | bytes 4194304
  449.6 24.9 %collective-permute-start.4 = (bf16[512,1536]{0,1:T(8,128)(2,1)}, bf16[512,1536]{0,1:T(8,128)(2,1)}, u32[]{:S(2)}, u32[]{:S(2)}) collective-permute-start(bf16[512,1536]{0,1:T(8,128)(2,1)} %pad_maximum_fusion.1), channel_id=1, source_target_pairs={{1,0},{2,1},{3,2},{4,3},{5,4},{6,5},{7,6},{8,7},{9,8},{10,9},{11,1... | collective-permute-start | bytes 4718600 | tf_op jit(solution)/shard_map/ppermute | solution.py:17
  452.2 79.3 %collective-permute-start.5 = (bf16[512,1536]{0,1:T(8,128)(2,1)}, bf16[512,1536]{0,1:T(8,128)(2,1)}, u32[]{:S(2)}, u32[]{:S(2)}) collective-permute-start(bf16[512,1536]{0,1:T(8,128)(2,1)} %pad_maximum_fusion.2), channel_id=1, source_target_pairs={{2,0},{3,1},{4,2},{5,3},{6,4},{7,5},{8,6},{9,7},{10,8},{11,9},{12,... | collective-permute-start | bytes 4718600 | tf_op jit(solution)/shard_map/ppermute | solution.py:17
  454.9 81.1 %collective-permute-start.6 = (bf16[512,1536]{0,1:T(8,128)(2,1)}, bf16[512,1536]{0,1:T(8,128)(2,1)}, u32[]{:S(2)}, u32[]{:S(2)}) collective-permute-start(bf16[512,1536]{0,1:T(8,128)(2,1)} %pad_maximum_fusion.3), channel_id=1, source_target_pairs={{3,0},{4,1},{5,2},{6,3},{7,4},{8,5},{9,6},{10,7},{11,8},{12,9},{13... | collective-permute-start | bytes 4718600 | tf_op jit(solution)/shard_map/ppermute | solution.py:17
  459.4 123.6 %collective-permute-start.7 = (bf16[512,1536]{0,1:T(8,128)(2,1)}, bf16[512,1536]{0,1:T(8,128)(2,1)}, u32[]{:S(2)}, u32[]{:S(2)}) collective-permute-start(bf16[512,1536]{0,1:T(8,128)(2,1)} %pad_maximum_fusion.4), channel_id=1, source_target_pairs={{4,0},{5,1},{6,2},{7,3},{8,4},{9,5},{10,6},{11,7},{12,8},{13,9},{1... | collective-permute-start | bytes 4718600 | tf_op jit(solution)/shard_map/ppermute | solution.py:17
  460.7 183.5 %reduce-scatter.5.cloned.1.call-start = ((), (), s32[]{:S(2)}) async-start(), calls=%async_computation.8 | async-start | bytes 4423680 | tf_op jit(solution)/shard_map/reduce_scatter | solution.py:253
  466.7 120.3 %copy-start.44 = (bf16[12,64,512]{2,1,0:T(8,128)(2,1)}, bf16[12,64,512]{2,1,0:T(8,128)(2,1)S(1)}, u32[]{:S(2)}) copy-start(bf16[12,64,512]{2,1,0:T(8,128)(2,1)S(1)} %multiply_convert_fusion.6) | copy-start | bytes 2359300
  474.4 113.6 %copy-start.8 = (bf16[512,768]{1,0:T(8,128)(2,1)S(1)}, bf16[512,768]{1,0:T(8,128)(2,1)}, u32[]{:S(2)}) copy-start(bf16[512,768]{1,0:T(8,128)(2,1)} %param.16) | copy-start | bytes 2359300
  474.5 113.6 %copy-start.64 = (f32[768]{0:T(1024)S(1)}, f32[768]{0:T(1024)}, u32[]{:S(2)}) copy-start(f32[768]{0:T(1024)} %copy-done.63) | copy-start | bytes 9220
  474.5 113.6 %copy-start.66 = (f32[512]{0:T(512)S(1)}, f32[512]{0:T(512)}, u32[]{:S(2)}) copy-start(f32[512]{0:T(512)} %copy-done.65) | copy-start | bytes 6148
  474.5 113.6 %copy-start.68 = (f32[512]{0:T(512)S(1)}, f32[512]{0:T(512)}, u32[]{:S(2)}) copy-start(f32[512]{0:T(512)} %copy-done.67) | copy-start | bytes 6148
  474.5 113.6 %copy-start.85 = (f32[768]{0:T(1024)S(1)}, f32[768]{0:T(1024)}, u32[]{:S(2)}) copy-start(f32[768]{0:T(1024)} %copy-done.84) | copy-start | bytes 9220
  592.3 92.1 %reduce-scatter.9.cloned.1.call-start = ((), (), s32[]{:S(2)}) async-start(), calls=%async_computation.10 | async-start | bytes 5898240 | tf_op jit(solution)/shard_map/reduce_scatter | solution.py:280
  598.9 136.0 %reduce-scatter.11.cloned.1.call-start = ((), (), s32[]{:S(2)}) async-start(), calls=%async_computation.11 | async-start | bytes 5898240 | tf_op jit(solution)/shard_map/reduce_scatter | solution.py:286
  612.3 19.4 %copy-start.6 = (f32[512,768]{1,0:T(8,128)S(1)}, f32[512,768]{1,0:T(8,128)}, u32[]{:S(2)}) copy-start(f32[512,768]{1,0:T(8,128)} %copy-done.5) | copy-start | bytes 4718596
  612.3 19.4 %copy-start.70 = (f32[512]{0:T(512)S(1)}, f32[512]{0:T(512)}, u32[]{:S(2)}) copy-start(f32[512]{0:T(512)} %copy-done.69) | copy-start | bytes 6148
  (89 other events, 559.6 us)
Sparse Core Ops, SparseCore 0:
  9.6 33.7 all-gather.5
  44.9 17.7 all-gather.7
  64.3 58.3 all-gather.9
  124.1 82.6 all-gather.11
  460.9 76.8 reduce-scatter.6
  592.4 41.4 reduce-scatter.4
  636.4 47.9 reduce-scatter.8
  687.1 47.8 reduce-scatter.10
where the time goes:
time: 1030 us; the launch traced here: 1020 us
  blocking collectives  350 us (34%)
  matrix products  253 us (25%)
  waiting for transfers between devices  211 us (20%)
  other arithmetic  99.3 us (10%)
  starting transfers between devices  46.3 us (4%)
  local copies, waits for them, and re-layouts  44.5 us (4%)
  between operations  17.9 us (2%)
    psum x1, blocking collectives, body(): lax.psum((shards[0], shards[1], shards[2], shards[3], shards[4], shards[5...  279 us
    ppermute x8, waiting for transfers between devices, from_behind(): lax.ppermute(value, axis, [(source, source + steps) for source in range(f...  109 us
    dot_general x5, matrix products, piece_slopes(): jnp.einsum('qhd,khd->hqk', grad_mixed, value_list[distance], preferred_el...  68.1 us
    convert_element_type x1, other arithmetic, body(): (weights * (piece_slopes(distance) - row_dots)).astype(jnp.bfloat16)  51.1 us
    reduce_scatter x1, waiting for transfers between devices, body(): lax.psum_scatter(local_grads[11].astype(jnp.bfloat16), 'shard', scatter_d...  50.6 us
    ppermute x8, starting transfers between devices, from_behind(): lax.ppermute(value, axis, [(source, source + steps) for source in range(f...  45.6 us
    all_gather x1, blocking collectives, body(): lax.all_gather(bias_up, 'shard', axis=0, tiled=True)  45.5 us
    reduce_scatter x1, waiting for transfers between devices, body(): lax.psum_scatter(local_grads[9].astype(jnp.bfloat16), 'shard', scatter_di...  40.2 us
  transfers between devices with their start and end apart: 16, of which 6 were waited for; matrix products, arithmetic and copies ran while one was open for 20% of the time, Pallas kernels for 0%

commit v1 on v0

v1 whole, which is shorter than its diff:
```python
import functools

import jax
import jax.numpy as jnp
from jax import lax
from jax.experimental import pallas as pl
from jax.experimental.pallas import tpu as pltpu
from jax.sharding import PartitionSpec as P

H = 12
GROUP = 8
TILE = 256

norm_eps = 1e-05
masked_value = -1e30


def layer_norm(values, gain, offset):
    centre = jnp.mean(values, axis=-1, keepdims=True)
    centred = values - centre
    variance = jnp.mean(centred * centred, axis=-1, keepdims=True)
    return centred * lax.rsqrt(variance + norm_eps) * gain + offset


def gelu_tanh(values):
    return jax.nn.gelu(values, approximate=True)


def dot(left, right, left_dim, right_dim):
    return lax.dot_general(
        left, right, (((left_dim,), (right_dim,)), ((), ())), preferred_element_type=jnp.float32
    )


def exchange_kernel(source, target, send_sem, recv_sem, local_sem):
    rep = lax.axis_index("rep")
    shard = lax.axis_index("shard")
    across = GROUP // 4
    base = rep // across * across
    me = (rep - base) * 4 + shard

    def place(index):
        return (base + index // 4, lax.rem(index, 4))

    barrier = pltpu.get_barrier_semaphore()
    for step in range(1, GROUP):
        pl.semaphore_signal(
            barrier,
            inc=1,
            device_id=place(lax.rem(me + step, GROUP)),
            device_id_type=pl.DeviceIdType.MESH,
        )
    pl.semaphore_wait(barrier, GROUP - 1)
    own = pltpu.make_async_copy(source.at[me], target.at[me], local_sem)
    own.start()
    copies = []
    for step in range(1, GROUP):
        peer = lax.rem(me + step, GROUP)
        copy = pltpu.make_async_remote_copy(
            src_ref=source.at[peer],
            dst_ref=target.at[me],
            send_sem=send_sem.at[step],
            recv_sem=recv_sem.at[step],
            device_id=place(peer),
            device_id_type=pl.DeviceIdType.MESH,
        )
        copy.start()
        copies.append(copy)
    own.wait()
    for copy in copies:
        copy.wait()


def exchange(blocks, number):
    return pl.pallas_call(
        exchange_kernel,
        out_shape=jax.ShapeDtypeStruct(blocks.shape, blocks.dtype),
        in_specs=[pl.BlockSpec(memory_space=pl.ANY)],
        out_specs=pl.BlockSpec(memory_space=pl.ANY),
        scratch_shapes=[
            pltpu.SemaphoreType.DMA((GROUP,)),
            pltpu.SemaphoreType.DMA((GROUP,)),
            pltpu.SemaphoreType.DMA,
        ],
        compiler_params=pltpu.CompilerParams(collective_id=number, has_side_effects=True),
        name="exchange",
    )(blocks)


def tile_mask(chunk, first_row, last_row):
    key_pos = chunk * TILE + lax.broadcasted_iota(jnp.int32, (TILE, TILE), 0)
    return (key_pos >= first_row) & (key_pos <= last_row)


def chunk_lanes(chunk, offset):
    return pl.ds(pl.multiple_of(lax.rem(chunk, 2) * TILE + offset, TILE), TILE)


def attend_kernel(heads, size, low_ref, high_ref, first_ref, last_ref, pack_ref, out_ref, lse_ref):
    step = pl.program_id(0)
    rows = pack_ref.shape[2] - TILE
    half = rows // 2
    first_row, last_row = first_ref[0], last_ref[0]
    high = high_ref[step]
    queries = [
        pack_ref[step, h * size : (h + 1) * size, rows:] * (size**-0.5) for h in range(heads)
    ]

    def work(turn, carry):
        chunk = high - turn
        block = chunk // 2
        mask = tile_mask(chunk, first_row, last_row)
        result = []
        for h in range(heads):
            top, total, mixed = carry[h]
            here = slice(h * size, (h + 1) * size)
            keys = pack_ref[block, here, chunk_lanes(chunk, 0)]
            values = pack_ref[block, here, chunk_lanes(chunk, half)]
            scores = jnp.where(mask, dot(keys, queries[h], 0, 0), masked_value)
            new_top = jnp.maximum(top, jnp.max(scores, axis=0, keepdims=True))
            fresh = jnp.exp(scores - new_top)
            fade = jnp.exp(top - new_top)
            total = total * fade + jnp.sum(fresh, axis=0, keepdims=True)
            mixed = mixed * fade + dot(values, fresh.astype(jnp.bfloat16), 1, 0)
            result.append((new_top, total, mixed))
        return tuple(result)

    start = tuple(
        (
            jnp.full((1, TILE), masked_value, jnp.float32),
            jnp.zeros((1, TILE), jnp.float32),
            jnp.zeros((size, TILE), jnp.float32),
        )
        for _ in range(heads)
    )
    done = lax.fori_loop(0, high - low_ref[step] + 1, work, start)
    for h in range(heads):
        top, total, mixed = done[h]
        out_ref[0, h * size : (h + 1) * size, :] = mixed / total
        lse_ref[0, h : h + 1, :] = top + jnp.log(total)


def attend(low, high, first, last, pack, heads, size):
    blocks, rows, lanes = pack.shape
    row_spec = pl.BlockSpec((1, 1, TILE), lambda i, *_: (i, 0, 0))
    return pl.pallas_call(
        functools.partial(attend_kernel, heads, size),
        out_shape=(
            jax.ShapeDtypeStruct((blocks, rows, TILE), jnp.float32),
            jax.ShapeDtypeStruct((blocks, 8, TILE), jnp.float32),
        ),
        grid_spec=pltpu.PrefetchScalarGridSpec(
            num_scalar_prefetch=2,
            grid=(blocks,),
            in_specs=[
                row_spec,
                row_spec,
                pl.BlockSpec((blocks, rows, lanes), lambda i, *_: (0, 0, 0)),
            ],
            out_specs=(
                pl.BlockSpec((1, rows, TILE), lambda i, *_: (i, 0, 0)),
                pl.BlockSpec((1, 8, TILE), lambda i, *_: (i, 0, 0)),
            ),
        ),
        compiler_params=pltpu.CompilerParams(vmem_limit_bytes=40 * 1024 * 1024),
        cost_estimate=pl.CostEstimate(
            flops=4 * heads * size * TILE * TILE * 40,
            bytes_accessed=pack.size * 2,
            transcendentals=heads * TILE * TILE * 40,
        ),
        name="attend",
    )(low, high, first, last, pack)


def attend_back_kernel(
    heads, size, low_ref, high_ref, first_ref, last_ref, pack_ref, slope_ref, mixed_ref, lse_ref,
    out_ref, total_ref,
):
    step = pl.program_id(0)
    rows = pack_ref.shape[2] - TILE
    half = rows // 2
    scale = size**-0.5
    first_row, last_row = first_ref[0], last_ref[0]
    high = high_ref[step]

    @pl.when(step == 0)
    def _():
        total_ref[...] = jnp.zeros_like(total_ref)

    places = [slice(h * size, (h + 1) * size) for h in range(heads)]
    queries = [pack_ref[step, here, rows:] * scale for here in places]
    incoming = [slope_ref[0, here, :] for here in places]
    row_dots = [
        jnp.sum(
            slope_ref[0, here, :].astype(jnp.float32) * mixed_ref[0, here, :], axis=0, keepdims=True
        )
        for here in places
    ]
    totals = [lse_ref[0, h : h + 1, :] for h in range(heads)]

    def work(turn, carry):
        chunk = high - turn
        block = chunk // 2
        mask = tile_mask(chunk, first_row, last_row)
        key_lanes, value_lanes = chunk_lanes(chunk, 0), chunk_lanes(chunk, half)
        result = []
        for h in range(heads):
            here = places[h]
            keys = pack_ref[block, here, key_lanes]
            values = pack_ref[block, here, value_lanes]
            scores = dot(keys, queries[h], 0, 0)
            weights = jnp.exp(jnp.where(mask, scores - totals[h], masked_value))
            slopes = dot(values, incoming[h], 0, 0)
            grad_scores = (weights * (slopes - row_dots[h])).astype(jnp.bfloat16)
            total_ref[block, here, value_lanes] += dot(
                incoming[h], weights.astype(jnp.bfloat16), 1, 1
            )
            total_ref[block, here, key_lanes] += dot(queries[h], grad_scores, 1, 1)
            result.append(carry[h] + dot(keys, grad_scores, 1, 0))
        return tuple(result)

    start = tuple(jnp.zeros((size, TILE), jnp.float32) for _ in range(heads))
    done = lax.fori_loop(0, high - low_ref[step] + 1, work, start)
    for h in range(heads):
        out_ref[step, places[h], rows:] = (done[h] * scale).astype(out_ref.dtype)

    @pl.when(step == pl.num_programs(0) - 1)
    def _():
        for block in range(out_ref.shape[0]):
            out_ref[block, :, :rows] = total_ref[block].astype(out_ref.dtype)


def attend_back(low, high, first, last, pack, slope, mixed, lse, heads, size):
    blocks, rows, lanes = pack.shape
    row_spec = pl.BlockSpec((1, 1, TILE), lambda i, *_: (i, 0, 0))
    whole = pl.BlockSpec((blocks, rows, lanes), lambda i, *_: (0, 0, 0))
    tile_spec = pl.BlockSpec((1, rows, TILE), lambda i, *_: (i, 0, 0))
    return pl.pallas_call(
        functools.partial(attend_back_kernel, heads, size),
        out_shape=jax.ShapeDtypeStruct(pack.shape, jnp.bfloat16),
        grid_spec=pltpu.PrefetchScalarGridSpec(
            num_scalar_prefetch=2,
            grid=(blocks,),
            in_specs=[
                row_spec,
                row_spec,
                whole,
                tile_spec,
                tile_spec,
                pl.BlockSpec((1, 8, TILE), lambda i, *_: (i, 0, 0)),
            ],
            out_specs=whole,
            scratch_shapes=[pltpu.VMEM((blocks, rows, lanes - TILE), jnp.float32)],
        ),
        compiler_params=pltpu.CompilerParams(vmem_limit_bytes=40 * 1024 * 1024),
        cost_estimate=pl.CostEstimate(
            flops=10 * heads * size * TILE * TILE * 40,
            bytes_accessed=pack.size * 4,
            transcendentals=heads * TILE * TILE * 40,
        ),
        name="attend_back",
    )(low, high, first, last, pack, slope, mixed, lse)


def reduce_weight(grad):
    part = lax.psum_scatter(
        grad.astype(jnp.bfloat16), "shard", scatter_dimension=0, tiled=True
    )
    count = lax.axis_size("rep")
    rows, columns = part.shape
    part = lax.psum_scatter(
        part.reshape(count, rows * columns // count // 768, 768), "rep", scatter_dimension=0,
        tiled=False,
    )
    return lax.all_gather(part, "rep", axis=0, tiled=False).reshape(rows, columns)


def body(
    tokens,
    cotangent,
    segment,
    w_qkv,
    bias_query,
    bias_value,
    w_out,
    bias_out,
    ln1_gain,
    ln1_bias,
    ln2_gain,
    ln2_bias,
    w_up,
    bias_up,
    w_down,
    bias_down,
):
    f32, bf16 = jnp.float32, jnp.bfloat16
    small = (
        bias_query, bias_value, bias_out, ln1_gain, ln1_bias, ln2_gain, ln2_bias, bias_down, bias_up,
    )
    sizes = [value.shape[0] for value in small]
    joined = lax.all_gather(jnp.concatenate(small), "shard", axis=0, tiled=False)
    full_small = []
    at = 0
    for length in sizes:
        full_small.append(joined[:, at : at + length].reshape(-1).astype(f32))
        at += length
    (
        query_bias, value_bias, out_bias, gain_one, offset_one, gain_two, offset_two, down_bias, up_bias,
    ) = full_small
    full_qkv = lax.all_gather(w_qkv, "shard", axis=0, tiled=True)
    full_wout = lax.all_gather(w_out, "shard", axis=0, tiled=True)
    full_wup = lax.all_gather(w_up, "shard", axis=0, tiled=True)
    full_wdown = lax.all_gather(w_down, "shard", axis=0, tiled=True)

    tok_rows, width = tokens.shape
    size = width // H
    shards = lax.axis_size("shard")
    heads = H // shards
    part = heads * size
    rep, shard = lax.axis_index("rep"), lax.axis_index("shard")
    halves = GROUP // shards
    side = lax.rem(rep, halves)
    parity = lax.rem(shard, 2)

    span = GROUP * tok_rows
    group_seg = lax.dynamic_slice_in_dim(segment, rep // halves * span, span, 0)
    one = jnp.sum((group_seg == group_seg[0]).astype(jnp.int32))
    two = span - jnp.sum((group_seg == group_seg[span - 1]).astype(jnp.int32))
    blocks = jnp.arange(GROUP, dtype=jnp.int32)
    high = 2 * blocks + jnp.where(blocks % 2 == 0, side, 1 - side)
    last = high[:, None] * TILE + jnp.arange(TILE, dtype=jnp.int32)[None, :]
    first = jnp.where(last >= two, two, jnp.where(last >= one, one, 0))
    low = first[:, 0] // TILE
    first, last = first[:, None, :], last[:, None, :]

    inputs = tokens.astype(f32)
    normed, norm_one_back = jax.vjp(layer_norm, inputs, gain_one, offset_one)
    normed_low = normed.astype(bf16)
    joined_bias = jnp.concatenate([query_bias, jnp.zeros_like(query_bias), value_bias])
    projected = (dot(full_qkv, normed_low, 0, 1) + joined_bias[:, None]).astype(bf16)
    parts = projected.reshape(3, shards, part, tok_rows)

    def by_side(value):
        near, far = value[..., :TILE], value[..., TILE:]
        swap = parity == 1
        return jnp.stack([jnp.where(swap, far, near), jnp.where(swap, near, far)], axis=0)

    def by_token(value):
        swap = parity == 1
        return jnp.concatenate(
            [jnp.where(swap, value[1], value[0]), jnp.where(swap, value[0], value[1])], axis=-1
        )

    pairs = jnp.concatenate([parts[1], parts[2]], axis=-1)
    message = jnp.concatenate(
        [jnp.broadcast_to(pairs[None], (halves,) + pairs.shape), by_side(parts[0])], axis=-1
    ).reshape(GROUP, part, 2 * tok_rows + TILE)
    pack = exchange(message, 1)
    mixed_tiles, lse = attend(low, high, first, last, pack, heads, size)
    back = exchange(mixed_tiles.astype(bf16), 2)
    mixed_low = by_token(back.reshape(halves, shards, part, TILE)).reshape(width, tok_rows)

    middle = inputs + dot(mixed_low, full_wout, 0, 0) + out_bias
    second, norm_two_back = jax.vjp(layer_norm, middle, gain_two, offset_two)
    second_low = second.astype(bf16)
    hidden = dot(second_low, full_wup, 1, 0) + up_bias
    active, gelu_back = jax.vjp(gelu_tanh, hidden)
    active_low = active.astype(bf16)
    layer_out = middle + dot(active_low, full_wdown, 1, 0) + down_bias
    grad_out = cotangent.astype(f32)
    grad_wdown = reduce_weight(dot(active_low, cotangent, 0, 0))
    grad_down_bias = jnp.sum(grad_out, axis=0)
    (grad_hidden,) = gelu_back(dot(cotangent, full_wdown, 1, 1))
    hidden_low = grad_hidden.astype(bf16)
    grad_wup = reduce_weight(dot(second_low, hidden_low, 0, 0))
    grad_up_bias = jnp.sum(hidden_low.astype(f32), axis=0)
    grad_second = dot(hidden_low, full_wup, 1, 1)
    grad_middle_norm, grad_gain_two, grad_offset_two = norm_two_back(grad_second)
    grad_middle = grad_out + grad_middle_norm
    middle_low = grad_middle.astype(bf16)
    grad_wout = reduce_weight(dot(mixed_low, middle_low, 1, 0))
    grad_out_bias = jnp.sum(middle_low.astype(f32), axis=0)
    grad_mixed = dot(full_wout, middle_low, 1, 1).astype(bf16)

    slope = exchange(
        by_side(grad_mixed.reshape(shards, part, tok_rows)).reshape(GROUP, part, TILE), 3
    )
    grad_pack = attend_back(low, high, first, last, pack, slope, mixed_tiles, lse, heads, size)
    returned = exchange(grad_pack, 4).reshape(halves, shards, part, 2 * tok_rows + TILE)
    grad_pairs = jnp.sum(returned[..., : 2 * tok_rows].astype(f32), axis=0).astype(bf16)
    grad_projected = jnp.stack(
        [
            by_token(returned[..., 2 * tok_rows :]),
            grad_pairs[..., :tok_rows],
            grad_pairs[..., tok_rows:],
        ],
        axis=0,
    ).reshape(3 * width, tok_rows)
    grad_wqkv = reduce_weight(dot(normed_low, grad_projected, 0, 1))
    bias_grads = jnp.sum(grad_projected.astype(f32), axis=1)
    grad_query_bias = bias_grads[:width]
    grad_value_bias = bias_grads[2 * width :]
    grad_normed = dot(grad_projected, full_qkv, 0, 1)
    grad_input_norm, grad_gain_one, grad_offset_one = norm_one_back(grad_normed)
    grad_input = grad_middle + grad_input_norm

    small_grads = (
        grad_query_bias, grad_value_bias, grad_out_bias, grad_gain_one, grad_offset_one,
        grad_gain_two, grad_offset_two, grad_down_bias, grad_up_bias,
    )
    laid = jnp.concatenate([value.reshape(shards, -1) for value in small_grads], axis=1)
    summed = lax.dynamic_index_in_dim(
        lax.psum(laid, ("rep", "shard")), shard, 0, keepdims=False
    )
    pieces = []
    at = 0
    for length in sizes:
        pieces.append(summed[at : at + length])
        at += length
    (
        sum_query_bias, sum_value_bias, sum_out_bias, sum_gain_one, sum_offset_one, sum_gain_two,
        sum_offset_two, sum_down_bias, sum_up_bias,
    ) = pieces
    return (
        layer_out,
        grad_input,
        grad_wqkv.astype(f32),
        sum_query_bias,
        sum_value_bias,
        grad_wout.astype(f32),
        sum_out_bias,
        sum_gain_one,
        sum_offset_one,
        sum_gain_two,
        sum_offset_two,
        grad_wup.astype(f32),
        sum_up_bias,
        grad_wdown.astype(f32),
        sum_down_bias,
    )


def solution(mesh):
    tokens_at, rows_at, vector_at = P(("rep", "shard"), None), P("shard", None), P("shard")
    return jax.shard_map(
        body,
        mesh=mesh,
        in_specs=(
            tokens_at, tokens_at, P(), rows_at, vector_at, vector_at, rows_at, vector_at, vector_at,
            vector_at, vector_at, vector_at, rows_at, vector_at, rows_at, vector_at,
        ),
        out_specs=(
            tokens_at, tokens_at, rows_at, vector_at, vector_at, rows_at, vector_at, vector_at,
            vector_at, vector_at, vector_at, rows_at, vector_at, rows_at, vector_at,
        ),
        check_vma=False,
    )
```

time: 1030 us -> 773 us (0.75)
  blocking collectives: 350 us -> 111 us
  Pallas kernels: 0 us -> 207 us
  matrix products: 253 us -> 68.7 us
  waiting for transfers between devices: 211 us -> 308 us
  other arithmetic: 99.3 us -> 25.1 us
  starting transfers between devices: 46.3 us -> 0.94 us
  local copies, waits for them, and re-layouts: 44.5 us -> 32.7 us
    psum x1, blocking collectives: 279 us -> 40.6 us  [body(): lax.psum(laid, ('rep', 'shard'))]
    pallas_call x0 -> x6, Pallas kernels: none -> 207 us  [the longest x4 150 us: exchange(): pl.pallas_call(exchange_kernel, out_shape=jax.ShapeDtypeStruct(blocks.sha...]
    dot_general x42 -> x12, matrix products: 253 us -> 68.7 us  [dot(): lax.dot_general(left, right, (((left_dim,), (right_dim,)), ((), ())), pre...]
    reduce_scatter x4 -> x8, waiting for transfers between devices: 90.7 us -> 226 us  [the longest x4 165 us: reduce_weight(): lax.psum_scatter(part.reshape(count, rows * columns // count // 768, 768)...]
    ppermute x8 -> x0, waiting for transfers between devices: 109 us -> none  [from_behind(): lax.ppermute(value, axis, [(source, source + steps) for source in range(f...]
    all_gather x4 -> x6, waiting for transfers between devices: 9.01 us -> 78.7 us  [the longest x2 49.5 us: reduce_weight(): lax.all_gather(part, 'rep', axis=0, tiled=False).reshape(rows, columns)]
    convert_element_type x18 -> x5, other arithmetic: 53.1 us -> 4.76 us  [the longest x1 2.85 us: body(): grad_wdown.astype(f32)]
    ppermute x8 -> x0, starting transfers between devices: 45.6 us -> none  [from_behind(): lax.ppermute(value, axis, [(source, source + steps) for source in range(f...]
  transfers between devices with their start and end apart: 16 -> 14, of which waited for: 6 -> 10; matrix products, arithmetic and copies ran while one was open for 20% -> 12% of each run, Pallas kernels for 0% -> 27%
where the time goes in v1:
time: 773 us; the launch traced here: 769 us
  waiting for transfers between devices  308 us (40%)
  Pallas kernels  207 us (27%)
  blocking collectives  111 us (14%)
  matrix products  68.7 us (9%)
  local copies, waits for them, and re-layouts  32.7 us (4%)
  other arithmetic  25.1 us (3%)
  between operations  15.4 us (2%)
    reduce_scatter x4, waiting for transfers between devices, reduce_weight(): lax.psum_scatter(part.reshape(count, rows * columns // count // 768, 768)...  165 us
    pallas_call x4, Pallas kernels, exchange(): pl.pallas_call(exchange_kernel, out_shape=jax.ShapeDtypeStruct(blocks.sha...  150 us
    dot_general x12, matrix products, dot(): lax.dot_general(left, right, (((left_dim,), (right_dim,)), ((), ())), pre...  68.7 us
    all_gather x2, blocking collectives, reduce_weight(): lax.all_gather(part, 'rep', axis=0, tiled=False).reshape(rows, columns)  64.2 us
    reduce_scatter x4, waiting for transfers between devices, reduce_weight(): lax.psum_scatter(grad.astype(jnp.bfloat16), 'shard', scatter_dimension=0,...  61.1 us
    all_gather x2, waiting for transfers between devices, reduce_weight(): lax.all_gather(part, 'rep', axis=0, tiled=False).reshape(rows, columns)  49.5 us
    psum x1, blocking collectives, body(): lax.psum(laid, ('rep', 'shard'))  40.6 us
    pallas_call x1, Pallas kernels, attend(): pl.pallas_call(functools.partial(attend_kernel, heads, size), out_shape=(...  28.6 us
  transfers between devices with their start and end apart: 14, of which 10 were waited for; matrix products, arithmetic and copies ran while one was open for 12% of the time, Pallas kernels for 27%

profile of v1, /device:TPU:0, one launch (start us, length us, event | category | flops | bytes accessed | tf_op | source)
XLA Modules:
  0.0 768.9 jit_solution(3886122491847958320)
XLA Ops:
  10.3 6.2 all-gather.1
  16.7 1.3 fusion.37
  18.0 2.7 convert_reduce_fusion.5
  23.8 19.4 %all-gather.9.cloned.1.call-done = bf16[768,2304]{1,0:T(8,128)(2,1)} async-done(((bf16[192,2304]{1,0:T(8,128)(2,1)}), bf16[768,2304]{1,0:T(8,128)(2,1)}) %all-gather.9.cloned.1.call-update) | async-done | bytes 3538960 | tf_op jit(solution)/shard_map/all_gather | solution.py:310
  43.2 4.2 fusion.8
  50.8 2.6 maximum_maximum_fusion
  53.5 50.3 %exchange.4.pack_ref = bf16[8,192,1280]{2,1,0:T(8,128)(2,1)} custom-call(bf16[8,192,1280]{2,1,0:T(8,128)(2,1)} %bitcast.80), custom_call_target="tpu_custom_call" | custom-call | tf_op jit(solution)/shard_map/exchange/pallas_call | solution.py:75
  103.8 2.1 copy-done
  105.9 28.6 %attend.1 = (f32[8,192,256]{2,1,0:T(8,128)S(1)}, f32[8,8,256]{2,1,0:T(8,128)S(1)}) custom-call(s32[8]{0:T(128)S(1)} %and_select_fusion.low_ref, s32[8]{0:T(128)S(1)} %get-tuple-element.37.high_ref, s32[8,1,256]{2,1,0:T(1,128)S(1)} %get-tuple-element.74.first_ref, s32[8,1,256]{2,1,0:T(1,128)S(1)} %get-tuple-element.73.last_ref, bf16[8,192,1280]{2,1,0:T(8,128)(2,1)S(1)} %copy-done), custom_call_target="tpu_custom_call" | custom-call | flops 2013265920 | bytes 3932160 | tf_op jit(solution)/shard_map/attend/pallas_call | solution.py:146
  135.5 17.5 %exchange.5 = bf16[8,192,256]{2,1,0:T(8,128)(2,1)} custom-call(bf16[8,192,256]{2,1,0:T(8,128)(2,1)} %convert_element_type.186.source), custom_call_target="tpu_custom_call" | custom-call | tf_op jit(solution)/shard_map/exchange/pallas_call | solution.py:75
  155.1 2.4 fusion.39
  159.0 8.2 %fusion.30 = f32[512,3072]{1,0:T(8,128)} fusion(bf16[768,3072]{1,0:T(8,128)(2,1)} %all-gather.13.cloned.1.call-done, f32[512,768]{1,0:T(8,128)} %copy-done.6, f32[768]{0:T(1024)S(1)} %reshape.356, f32[768]{0:T(1024)S(1)} %reshape.355, f32[512]{0:T(512)S(1)} %fusion.24, f32[512]{0:T(512)S(1)} %broadcast_multiply_fusion), kind=kOutput, calls=%fused_computation.110 | convolution fusion | flops 2417885184 | bytes 12593152 | tf_op jit(solution)/shard_map/dot_general | solution.py:30
  167.2 9.9 %all-gather.15.cloned.1.call-done = bf16[3072,768]{1,0:T(8,128)(2,1)} async-done(((bf16[768,768]{1,0:T(8,128)(2,1)}), bf16[3072,768]{1,0:T(8,128)(2,1)}) %all-gather.15.cloned.1.call-update) | async-done | bytes 4718608 | tf_op jit(solution)/shard_map/all_gather | solution.py:313
  177.1 9.1 %convert_reduce_fusion = (f32[3072]{0:T(1024)S(1)}, bf16[512,3072]{1,0:T(8,128)(2,1)S(1)}) fusion(f32[512,3072]{1,0:T(8,128)} %fusion.30, f32[3072]{0:T(1024)S(1)} %reshape.357, bf16[512,768]{1,0:T(8,128)(2,1)} %param.17, bf16[3072,768]{1,0:T(8,128)(2,1)} %all-gather.15.cloned.1.call-done), kind=kOutput, calls=%fused_computation.9 | convolution fusion | flops 2452091904 | bytes 14966784 | tf_op jit(solution)/shard_map/dot_general | solution.py:30
  186.2 1.6 copy-done.24
  187.8 4.9 convolution_convert_fusion.1
  193.0 9.5 %convolution_convert_fusion = bf16[3072,768]{1,0:T(8,128)(2,1)} fusion(bf16[512,768]{1,0:T(8,128)(2,1)} %param.17, f32[512,3072]{1,0:T(8,128)} %fusion.30, f32[3072]{0:T(1024)S(1)} %reshape.357), kind=kOutput, calls=%fused_computation.11 | convolution fusion | flops 2434007040 | bytes 11808768 | tf_op jit(solution)/shard_map/dot_general | solution.py:30
  202.6 6.7 multiply_reduce_fusion
  211.7 1.7 fusion.21
  213.4 2.3 copy.41
  215.7 3.2 convolution_convert_fusion.3
  221.3 15.3 %exchange.6.slope_ref = bf16[8,192,256]{2,1,0:T(8,128)(2,1)} custom-call(bf16[8,192,256]{2,1,0:T(8,128)(2,1)} %bitcast.83), custom_call_target="tpu_custom_call" | custom-call | tf_op jit(solution)/shard_map/exchange/pallas_call | solution.py:75
  236.5 2.1 copy-done.1
  239.8 28.5 %attend_back.1.source = bf16[8,192,1280]{2,1,0:T(8,128)(2,1)S(1)} custom-call(s32[8]{0:T(128)S(1)} %and_select_fusion.low_ref, s32[8]{0:T(128)S(1)} %get-tuple-element.37.high_ref, s32[8,1,256]{2,1,0:T(1,128)S(1)} %get-tuple-element.74.first_ref, s32[8,1,256]{2,1,0:T(1,128)S(1)} %get-tuple-element.73.last_ref, bf16[8,192,1280]{2,1,0:T(8,128)(2,1)S(1)} %copy-done.1, ...), custom_call_target="tpu_custom_call" | custom-call | flops 5033164800 | bytes 7864320 | tf_op jit(solution)/shard_map/attend_back/pallas_call | solution.py:238
  268.3 1.9 copy-done.2
  270.2 67.0 %exchange.7 = bf16[8,192,1280]{2,1,0:T(8,128)(2,1)} custom-call(bf16[8,192,1280]{2,1,0:T(8,128)(2,1)} %copy-done.2), custom_call_target="tpu_custom_call" | custom-call | tf_op jit(solution)/shard_map/exchange/pallas_call | solution.py:75
  338.4 2.7 slice_reduce_fusion
  341.9 1.4 copy-done.12
  343.3 4.1 convolution_convert_fusion.2
  347.5 3.1 reshape.348
  351.3 18.0 %reduce-scatter.13.cloned.1.call-done = bf16[192,768]{1,0:T(8,128)(2,1)} async-done(((bf16[768,768]{1,0:T(8,128)(2,1)}), bf16[192,768]{1,0:T(8,128)(2,1)}) %reduce-scatter.13.cloned.1.call-update) | async-done | bytes 294928 | tf_op jit(solution)/shard_map/reduce_scatter | solution.py:266
  369.3 43.1 %reduce-scatter.9.cloned.1.call-done = bf16[192,2304]{1,0:T(8,128)(2,1)} async-done(((bf16[768,2304]{1,0:T(8,128)(2,1)}), bf16[192,2304]{1,0:T(8,128)(2,1)}) %reduce-scatter.9.cloned.1.call-update) | async-done | bytes 884752 | tf_op jit(solution)/shard_map/reduce_scatter | solution.py:266
  412.5 2.2 reshape.339
  414.8 65.7 %reduce-scatter.19.cloned.1.call-done = bf16[1,96,768]{2,1,0:T(8,128)(2,1)} async-done(((bf16[8,96,768]{2,1,0:T(8,128)(2,1)}), bf16[1,96,768]{2,1,0:T(8,128)(2,1)}) %reduce-scatter.19.cloned.1.call-update) | async-done | bytes 147472 | tf_op jit(solution)/shard_map/reduce_scatter | solution.py:271
  480.6 5.0 fusion.31
  486.7 1.9 convert_reduce_fusion.3
  488.6 58.1 %reduce-scatter.23.cloned.1.call-done = bf16[1,96,768]{2,1,0:T(8,128)(2,1)} async-done(((bf16[8,96,768]{2,1,0:T(8,128)(2,1)}), bf16[1,96,768]{2,1,0:T(8,128)(2,1)}) %reduce-scatter.23.cloned.1.call-update) | async-done | bytes 147472 | tf_op jit(solution)/shard_map/reduce_scatter | solution.py:271
  547.4 40.6 %psum.7 = f32[4,2304]{1,0:T(4,128)S(1)} all-reduce(f32[4,2304]{1,0:T(4,128)S(1)} %concatenate.27), channel_id=1, replica_groups=mesh['rep'=8,'shard'=4] {'rep','shard'}, use_global_device_ids=true, to_apply=%region_21.22 | all-reduce | flops 9216 | bytes 73728 | tf_op jit(solution)/shard_map/psum | solution.py:413
  589.3 9.7 %add_add_fusion.3 = f32[512,768]{1,0:T(8,128)} fusion(f32[512,768]{1,0:T(8,128)} %copy-done.6, bf16[3072,768]{1,0:T(8,128)(2,1)} %all-gather.15.cloned.1.call-done, f32[768]{0:T(1024)S(1)} %reshape.358, f32[512,3072]{1,0:T(8,128)} %fusion.30, f32[3072]{0:T(1024)S(1)} %reshape.357), kind=kOutput, calls=%fused_computation.45 | convolution fusion | flops 2432434176 | bytes 14171136 | tf_op jit(solution)/shard_map/dot_general | solution.py:30
  599.0 8.8 %reduce-scatter.15.cloned.1.call-done = bf16[1,24,768]{2,1,0:T(8,128)(2,1)} async-done(((bf16[8,24,768]{2,1,0:T(8,128)(2,1)}), bf16[1,24,768]{2,1,0:T(8,128)(2,1)}) %reduce-scatter.15.cloned.1.call-update) | async-done | bytes 36880 | tf_op jit(solution)/shard_map/reduce_scatter | solution.py:271
  607.9 31.5 %all_gather.37 = bf16[8,24,768]{2,1,0:T(8,128)(2,1)S(1)} all-gather(bf16[1,24,768]{2,1,0:T(8,128)(2,1)} %reduce-scatter.15.cloned.1.call-done), channel_id=1, replica_groups=mesh['rep'=8,'shard'=4] {'rep'}, dimensions={0}, use_global_device_ids=true | all-gather | bytes 331776 | tf_op jit(solution)/shard_map/all_gather | solution.py:275
  640.2 32.2 %reduce-scatter.11.cloned.1.call-done = bf16[1,72,768]{2,1,0:T(8,128)(2,1)} async-done(((bf16[8,72,768]{2,1,0:T(8,128)(2,1)}), bf16[1,72,768]{2,1,0:T(8,128)(2,1)}) %reduce-scatter.11.cloned.1.call-update) | async-done | bytes 110608 | tf_op jit(solution)/shard_map/reduce_scatter | solution.py:271
  672.4 32.7 %all_gather.36 = bf16[8,72,768]{2,1,0:T(8,128)(2,1)S(1)} all-gather(bf16[1,72,768]{2,1,0:T(8,128)(2,1)} %reduce-scatter.11.cloned.1.call-done), channel_id=1, replica_groups=mesh['rep'=8,'shard'=4] {'rep'}, dimensions={0}, use_global_device_ids=true | all-gather | bytes 995328 | tf_op jit(solution)/shard_map/all_gather | solution.py:275
  705.2 1.6 reshape.359
  706.7 10.5 %all-gather.17.cloned.1.call-done = bf16[8,96,768]{2,1,0:T(8,128)(2,1)} async-done(((bf16[1,96,768]{2,1,0:T(8,128)(2,1)}), bf16[8,96,768]{2,1,0:T(8,128)(2,1)}) %all-gather.17.cloned.1.call-update) | async-done | bytes 1179664 | tf_op jit(solution)/shard_map/all_gather | solution.py:275
  717.2 3.1 reshape.361
  720.4 38.9 %all-gather.19.cloned.1.call-done = bf16[8,96,768]{2,1,0:T(8,128)(2,1)} async-done(((bf16[1,96,768]{2,1,0:T(8,128)(2,1)}), bf16[8,96,768]{2,1,0:T(8,128)(2,1)}) %all-gather.19.cloned.1.call-update) | async-done | bytes 1179664 | tf_op jit(solution)/shard_map/all_gather | solution.py:275
  759.3 2.8 bitcast_convert_fusion
  (137 shorter events, 26.5 us)
Async XLA Ops:
  7.2 3.0 copy-start.15
  7.2 3.0 copy-start.16
  7.2 3.0 copy-start.17
  7.2 3.0 copy-start.18
  7.2 3.0 copy-start.19
  7.2 3.0 copy-start.20
  7.2 3.0 copy-start.21
  7.3 3.0 copy-start.22
  7.3 3.0 copy-start.14
  7.3 35.9 %all-gather.9.cloned.1.call-start = ((), (), s32[]{:S(2)}) async-start(), calls=%async_computation.8 | async-start | bytes 4423680 | tf_op jit(solution)/shard_map/all_gather | solution.py:310
  8.0 13.8 %copy-start.4 = (bf16[512,768]{1,0:T(8,128)(2,1)S(1)}, bf16[512,768]{1,0:T(8,128)(2,1)}, u32[]{:S(2)}) copy-start(bf16[512,768]{1,0:T(8,128)(2,1)} %param.16) | copy-start | bytes 2359300
  8.0 147.1 %all-gather.11.cloned.1.call-start = ((), (), s32[]{:S(2)}) async-start(), calls=%async_computation.9 | async-start | bytes 1474560 | tf_op jit(solution)/shard_map/all_gather | solution.py:311
  8.8 150.2 %all-gather.13.cloned.1.call-start = ((), (), s32[]{:S(2)}) async-start(), calls=%async_computation.10 | async-start | bytes 5898240 | tf_op jit(solution)/shard_map/all_gather | solution.py:312
  9.5 167.6 %all-gather.15.cloned.1.call-start = ((), (), s32[]{:S(2)}) async-start(), calls=%async_computation.11 | async-start | bytes 5898240 | tf_op jit(solution)/shard_map/all_gather | solution.py:313
  10.1 337.4 %reduce-scatter.17.cloned.1.call-start = ((), (), s32[]{:S(2)}) async-start(), calls=%async_computation.16 | async-start | bytes 5898240 | tf_op jit(solution)/shard_map/reduce_scatter | solution.py:266
  49.2 1.1 copy-start.9
  103.8 2.1 copy-start
  157.5 1.1 copy-start.6
  167.2 20.6 %copy-start.7 = (f32[512,768]{1,0:T(8,128)S(1)}, f32[512,768]{1,0:T(8,128)}, u32[]{:S(2)}) copy-start(f32[512,768]{1,0:T(8,128)} %copy-done.6) | copy-start | bytes 4718596
  186.2 1.6 copy-start.24
  192.8 157.9 %reduce-scatter.21.cloned.1.call-start = ((), (), s32[]{:S(2)}) async-start(), calls=%async_computation.19 | async-start | bytes 5898240 | tf_op jit(solution)/shard_map/reduce_scatter | solution.py:266
  202.5 166.7 %reduce-scatter.13.cloned.1.call-start = ((), (), s32[]{:S(2)}) async-start(), calls=%async_computation.14 | async-start | bytes 1474560 | tf_op jit(solution)/shard_map/reduce_scatter | solution.py:266
  202.6 6.7 copy-start.8
  209.3 1.1 copy-start.10
  210.4 1.3 copy-start.23
  210.8 0.9 copy-start.13
  218.9 193.6 %reduce-scatter.9.cloned.1.call-start = ((), (), s32[]{:S(2)}) async-start(), calls=%async_computation.12 | async-start | bytes 4423680 | tf_op jit(solution)/shard_map/reduce_scatter | solution.py:266
  236.5 2.1 copy-start.1
  238.7 1.1 copy-start.3
  268.3 1.9 copy-start.2
  341.4 1.9 copy-start.5
  341.9 1.4 copy-start.12
  347.4 133.0 %reduce-scatter.19.cloned.1.call-start = ((), (), s32[]{:S(2)}) async-start(), calls=%async_computation.17 | async-start | bytes 1327104 | tf_op jit(solution)/shard_map/reduce_scatter | solution.py:271
  350.7 196.1 %reduce-scatter.23.cloned.1.call-start = ((), (), s32[]{:S(2)}) async-start(), calls=%async_computation.20 | async-start | bytes 1327104 | tf_op jit(solution)/shard_map/reduce_scatter | solution.py:271
  351.3 256.6 %reduce-scatter.15.cloned.1.call-start = ((), (), s32[]{:S(2)}) async-start(), calls=%async_computation.15 | async-start | bytes 331776 | tf_op jit(solution)/shard_map/reduce_scatter | solution.py:271
  369.3 303.1 %reduce-scatter.11.cloned.1.call-start = ((), (), s32[]{:S(2)}) async-start(), calls=%async_computation.13 | async-start | bytes 995328 | tf_op jit(solution)/shard_map/reduce_scatter | solution.py:271
  414.7 302.5 %all-gather.17.cloned.1.call-start = ((), (), s32[]{:S(2)}) async-start(), calls=%async_computation.18 | async-start | bytes 1327104 | tf_op jit(solution)/shard_map/all_gather | solution.py:275
  480.5 278.8 %all-gather.19.cloned.1.call-start = ((), (), s32[]{:S(2)}) async-start(), calls=%async_computation.21 | async-start | bytes 1327104 | tf_op jit(solution)/shard_map/all_gather | solution.py:275
  485.6 1.1 copy-start.11
Sparse Core Ops, SparseCore 0:
  9.7 33.4 all-gather.8
  44.7 41.8 all-gather.10
  88.2 41.5 all-gather.12
  131.2 45.8 all-gather.14
  192.9 56.2 reduce-scatter.16
  251.8 89.9 reduce-scatter.20
  345.0 24.2 reduce-scatter.12
  372.0 40.4 reduce-scatter.8
  416.4 63.9 reduce-scatter.18
  483.7 63.0 reduce-scatter.22
  550.0 57.7 reduce-scatter.14
  611.7 60.6 reduce-scatter.10
  674.6 42.5 all-gather.16
  719.3 39.9 all-gather.18

commit v2 on v1

--- a/solution.py
+++ b/solution.py
@@ -262,17 +262,60 @@
     )(low, high, first, last, pack, slope, mixed, lse)
 
 
-def reduce_weight(grad):
-    part = lax.psum_scatter(
-        grad.astype(jnp.bfloat16), "shard", scatter_dimension=0, tiled=True
-    )
-    count = lax.axis_size("rep")
-    rows, columns = part.shape
-    part = lax.psum_scatter(
-        part.reshape(count, rows * columns // count // 768, 768), "rep", scatter_dimension=0,
-        tiled=False,
-    )
-    return lax.all_gather(part, "rep", axis=0, tiled=False).reshape(rows, columns)
+def swap_with(value, bit):
+    count = lax.axis_size(("rep", "shard"))
+    return lax.ppermute(
+        value, ("rep", "shard"), [(index, index ^ (1 << bit)) for index in range(count)]
+    )
+
+
+def bit_of(index, bit):
+    return lax.rem(index // (1 << bit), 2)
+
+
+def reduce_weight(grad, pieces=1, turned=False):
+    count = lax.axis_size(("rep", "shard"))
+    bits = count.bit_length() - 1
+    shards = lax.axis_size("shard")
+    shard_bits = shards.bit_length() - 1
+    index = lax.axis_index("rep") * shards + lax.axis_index("shard")
+    rows, columns = grad.shape
+    lanes = 768 // pieces
+    names = list(range(shard_bits - 1, -1, -1)) + list(range(bits - 1, shard_bits - 1, -1))
+    parts = grad.astype(jnp.bfloat16).reshape(
+        (2,) * bits + (rows * columns // count // 768, pieces, lanes)
+    )
+    done = []
+    for piece in range(pieces):
+        part = parts[..., piece, :]
+        left = list(names)
+        order = list(range(bits))
+        if (piece % 2 == 1) != turned:
+            order[1:3] = order[2:0:-1]
+        for bit in order:
+            axis = left.index(bit)
+            mine = bit_of(index, bit)
+            keep = lax.dynamic_index_in_dim(part, mine, axis, keepdims=False)
+            give = lax.dynamic_index_in_dim(part, 1 - mine, axis, keepdims=False)
+            came = swap_with(give, bit)
+            part = (keep.astype(jnp.float32) + came.astype(jnp.float32)).astype(jnp.bfloat16)
+            left.remove(bit)
+        for bit in range(bits - 1, shard_bits - 1, -1):
+            came = swap_with(part, bit)
+            mine = bit_of(index, bit)
+            axis = bits - 1 - bit
+            low = jnp.where(mine == 0, part, came)
+            high = jnp.where(mine == 0, came, part)
+            part = jnp.stack([low, high], axis=axis)
+        done.append(part)
+    whole = jnp.stack(done, axis=-2) if pieces > 1 else done[0]
+    return whole.reshape(rows // shards, columns)
+
+
+def reduce_small(value):
+    for bit in range(lax.axis_size(("rep", "shard")).bit_length() - 1):
+        value = value + swap_with(value, bit)
+    return value
 
 
 def body(
@@ -372,7 +415,7 @@
     grad_down_bias = jnp.sum(grad_out, axis=0)
     (grad_hidden,) = gelu_back(dot(cotangent, full_wdown, 1, 1))
     hidden_low = grad_hidden.astype(bf16)
-    grad_wup = reduce_weight(dot(second_low, hidden_low, 0, 0))
+    grad_wup = reduce_weight(dot(second_low, hidden_low, 0, 0), 1, True)
     grad_up_bias = jnp.sum(hidden_low.astype(f32), axis=0)
     grad_second = dot(hidden_low, full_wup, 1, 1)
     grad_middle_norm, grad_gain_two, grad_offset_two = norm_two_back(grad_second)
@@ -396,7 +439,7 @@
         ],
         axis=0,
     ).reshape(3 * width, tok_rows)
-    grad_wqkv = reduce_weight(dot(normed_low, grad_projected, 0, 1))
+    grad_wqkv = reduce_weight(dot(normed_low, grad_projected, 0, 1), 2)
     bias_grads = jnp.sum(grad_projected.astype(f32), axis=1)
     grad_query_bias = bias_grads[:width]
     grad_value_bias = bias_grads[2 * width :]
@@ -410,7 +453,7 @@
     )
     laid = jnp.concatenate([value.reshape(shards, -1) for value in small_grads], axis=1)
     summed = lax.dynamic_index_in_dim(
-        lax.psum(laid, ("rep", "shard")), shard, 0, keepdims=False
+        reduce_small(laid), shard, 0, keepdims=False
     )
     pieces = []
     at = 0

time: 773 us -> 579 us (0.75)
  waiting for transfers between devices: 308 us -> 132 us
  blocking collectives: 111 us -> 6.2 us
  starting transfers between devices: 0.94 us -> 58.2 us
  local copies, waits for them, and re-layouts: 32.7 us -> 77.9 us
  Pallas kernels: 207 us -> 183 us
  other arithmetic: 25.1 us -> 38.1 us
    reduce_scatter x8 -> x0, waiting for transfers between devices: 226 us -> none  [the longest x4 165 us: reduce_weight(): lax.psum_scatter(part.reshape(count, rows * columns // count // 768, 768)...]
    ppermute x0 -> x45, waiting for transfers between devices: none -> 102 us  [swap_with(): lax.ppermute(value, ('rep', 'shard'), [(index, index ^ 1 << bit) for inde...]
    all_gather x2 -> x0, blocking collectives: 64.2 us -> none  [reduce_weight(): lax.all_gather(part, 'rep', axis=0, tiled=False).reshape(rows, columns)]
    ppermute x0 -> x45, starting transfers between devices: none -> 58 us  [swap_with(): lax.ppermute(value, ('rep', 'shard'), [(index, index ^ 1 << bit) for inde...]
    all_gather x2 -> x0, waiting for transfers between devices: 49.5 us -> none  [reduce_weight(): lax.all_gather(part, 'rep', axis=0, tiled=False).reshape(rows, columns)]
    psum x1 -> x0, blocking collectives: 40.6 us -> none  [body(): lax.psum(laid, ('rep', 'shard'))]
    pallas_call x4, Pallas kernels: 150 us -> 125 us  [exchange(): pl.pallas_call(exchange_kernel, out_shape=jax.ShapeDtypeStruct(blocks.sha...]
    dynamic_slice x0 -> x4, local copies, waits for them, and re-layouts: none -> 10.2 us  [the longest x3 10.1 us: reduce_weight(): keep = lax.dynamic_index_in_dim(part, mine, axis, keepdims=False)]
  transfers between devices with their start and end apart: 14 -> 49, of which waited for: 10 -> 30; matrix products, arithmetic and copies ran while one was open for 12% -> 17% of each run, Pallas kernels for 27% -> 17%
where the time goes in v2:
time: 579 us; the launch traced here: 573 us
  Pallas kernels  183 us (32%)
  waiting for transfers between devices  132 us (23%)
  local copies, waits for them, and re-layouts  77.9 us (13%)
  matrix products  62.6 us (11%)
  starting transfers between devices  58.2 us (10%)
  other arithmetic  38.1 us (7%)
  between operations  16.2 us (3%)
  blocking collectives  6.2 us (1%)
    pallas_call x4, Pallas kernels, exchange(): pl.pallas_call(exchange_kernel, out_shape=jax.ShapeDtypeStruct(blocks.sha...  125 us
    ppermute x45, waiting for transfers between devices, swap_with(): lax.ppermute(value, ('rep', 'shard'), [(index, index ^ 1 << bit) for inde...  102 us
    dot_general x12, matrix products, dot(): lax.dot_general(left, right, (((left_dim,), (right_dim,)), ((), ())), pre...  62.6 us
    ppermute x45, starting transfers between devices, swap_with(): lax.ppermute(value, ('rep', 'shard'), [(index, index ^ 1 << bit) for inde...  58 us
    pallas_call x1, Pallas kernels, attend_back(): pl.pallas_call(functools.partial(attend_back_kernel, heads, size), out_sh...  28.9 us
    pallas_call x1, Pallas kernels, attend(): pl.pallas_call(functools.partial(attend_kernel, heads, size), out_shape=(...  28.6 us
    all_gather x1, waiting for transfers between devices, body(): full_qkv = lax.all_gather(w_qkv, 'shard', axis=0, tiled=True)  18.6 us
  transfers between devices with their start and end apart: 49, of which 30 were waited for; matrix products, arithmetic and copies ran while one was open for 17% of the time, Pallas kernels for 17%

profile of v2, /device:TPU:0, one launch (start us, length us, event | category | flops | bytes accessed | tf_op | source)
XLA Modules:
  0.0 573.5 jit_solution(14879266541267985497)
XLA Ops:
  10.4 6.2 %all-gather.1 = bf16[4,1,2304]{2,1,0:T(2,128)(2,1)S(1)} all-gather(bf16[1,1,2304]{2,1,0:T(2,128)(2,1)S(1)} %reshape.435), channel_id=2, replica_groups=mesh['rep'=8,'shard'=4] {'shard'}, dimensions={0}, use_global_device_ids=true | all-gather | bytes 23040 | tf_op jit(solution)/shard_map/all_gather | solution.py:344
  18.1 2.7 convert_reduce_fusion.5
  24.6 18.6 %all-gather.7.cloned.1.call-done = bf16[768,2304]{1,0:T(8,128)(2,1)} async-done(((bf16[192,2304]{1,0:T(8,128)(2,1)}), bf16[768,2304]{1,0:T(8,128)(2,1)}) %all-gather.7.cloned.1.call-update) | async-done | bytes 3538960 | tf_op jit(solution)/shard_map/all_gather | solution.py:353
  43.2 4.2 fusion.10
  54.3 48.7 %exchange.4.pack_ref = bf16[8,192,1280]{2,1,0:T(8,128)(2,1)} custom-call(bf16[8,192,1280]{2,1,0:T(8,128)(2,1)} %bitcast.278), custom_call_target="tpu_custom_call" | custom-call | tf_op jit(solution)/shard_map/exchange/pallas_call | solution.py:75
  105.1 28.6 %attend.1 = (f32[8,192,256]{2,1,0:T(8,128)S(1)}, f32[8,8,256]{2,1,0:T(8,128)S(1)}) custom-call(s32[8]{0:T(128)S(1)} %and_select_fusion.low_ref, s32[8]{0:T(128)S(1)} %get-tuple-element.37.high_ref, s32[8,1,256]{2,1,0:T(1,128)S(1)} %get-tuple-element.112.first_ref, s32[8,1,256]{2,1,0:T(1,128)S(1)} %get-tuple-element.111.last_ref, ...), custom_call_target="tpu_custom_call" | custom-call | flops 2013265920 | bytes 3932160 | tf_op jit(solution)/shard_map/attend/pallas_call | solution.py:146
  134.7 19.5 %exchange.5 = bf16[8,192,256]{2,1,0:T(8,128)(2,1)} custom-call(bf16[8,192,256]{2,1,0:T(8,128)(2,1)} %convert_element_type.486.source), custom_call_target="tpu_custom_call" | custom-call | tf_op jit(solution)/shard_map/exchange/pallas_call | solution.py:75
  155.5 3.5 fusion.66
  160.8 8.2 %fusion.56 = f32[512,3072]{1,0:T(8,128)} fusion(bf16[768,3072]{1,0:T(8,128)(2,1)} %all-gather.11.cloned.1.call-done, f32[512,768]{1,0:T(8,128)} %get-tuple-element.114, f32[768]{0:T(1024)S(1)} %reshape.402, f32[768]{0:T(1024)S(1)} %reshape.401, f32[512]{0:T(512)S(1)} %fusion.50, f32[512]{0:T(512)S(1)} %broadcast_multiply_fusion), kind=kOutput, calls=%fused_computation.240 | convolution fusion | flops 2417885184 | bytes 12593152 | tf_op jit(solution)/shard_map/dot_general | solution.py:30
  169.0 8.3 %all-gather.13.cloned.1.call-done = bf16[3072,768]{1,0:T(8,128)(2,1)} async-done(((bf16[768,768]{1,0:T(8,128)(2,1)}), bf16[3072,768]{1,0:T(8,128)(2,1)}) %all-gather.13.cloned.1.call-update) | async-done | bytes 4718608 | tf_op jit(solution)/shard_map/all_gather | solution.py:356
  177.3 9.9 %convert_reduce_fusion = (f32[3072]{0:T(1024)}, bf16[512,3072]{1,0:T(8,128)(2,1)S(1)}) fusion(f32[512,3072]{1,0:T(8,128)} %fusion.56, f32[3072]{0:T(1024)S(1)} %reshape.403, bf16[512,768]{1,0:T(8,128)(2,1)S(1)} %copy-done.8, bf16[3072,768]{1,0:T(8,128)(2,1)} %all-gather.13.cloned.1.call-done), kind=kOutput, calls=%fused_computation.9 | convolution fusion | flops 2452091904 | bytes 14966784 | tf_op jit(solution)/shard_map/dot_general | solution.py:30
  187.2 6.1 %multiply_reduce_fusion = (f32[768]{0:T(1024)}, f32[512]{0:T(512)S(1)}, f32[768]{0:T(1024)}, f32[512,768]{1,0:T(8,128)S(1)}) fusion(f32[512,768]{1,0:T(8,128)} %get-tuple-element.114, f32[512]{0:T(512)S(1)} %fusion.50, f32[512]{0:T(512)S(1)} %broadcast_multiply_fusion, f32[768]{0:T(1024)S(1)} %reshape.401, bf16[512,3072]{1,0:T(8,128)(2,1)S(1)} %get-tuple-element.29, ...), kind=kOutput, calls=%fused_computation.56 | convolution fusion | flops 2419062784 | bytes 11025408 | tf_op jit(solution)/shard_map/dot_general | solution.py:30
  202.7 10.9 %exchange.6.slope_ref = bf16[8,192,256]{2,1,0:T(8,128)(2,1)} custom-call(bf16[8,192,256]{2,1,0:T(8,128)(2,1)} %bitcast.282), custom_call_target="tpu_custom_call" | custom-call | tf_op jit(solution)/shard_map/exchange/pallas_call | solution.py:75
  216.9 28.9 %attend_back.1.source = bf16[8,192,1280]{2,1,0:T(8,128)(2,1)S(1)} custom-call(s32[8]{0:T(128)S(1)} %and_select_fusion.low_ref, s32[8]{0:T(128)S(1)} %get-tuple-element.37.high_ref, s32[8,1,256]{2,1,0:T(1,128)S(1)} %get-tuple-element.112.first_ref, s32[8,1,256]{2,1,0:T(1,128)S(1)} %get-tuple-element.111.last_ref, bf16[8,192,1280]{2,1,0:T(8,128)(2,1)S(1)} %copy-done.1, ...), custom_call_target="tpu_custom_call" | custom-call | flops 5033164800 | bytes 7864320 | tf_op jit(solution)/shard_map/attend_back/pallas_call | solution.py:238
  247.7 46.0 %exchange.7 = bf16[8,192,1280]{2,1,0:T(8,128)(2,1)} custom-call(bf16[8,192,1280]{2,1,0:T(8,128)(2,1)} %copy-done.2), custom_call_target="tpu_custom_call" | custom-call | tf_op jit(solution)/shard_map/exchange/pallas_call | solution.py:75
  293.7 2.8 slice_reduce_fusion
  300.0 6.2 %convolution_convert_fusion.1 = bf16[768,3072]{1,0:T(8,128)(2,1)} fusion(bf16[512,3072]{1,0:T(8,128)(2,1)S(1)} %copy-done.34, f32[512,768]{1,0:T(8,128)} %get-tuple-element.114, f32[768]{0:T(1024)S(1)} %reshape.402, f32[768]{0:T(1024)S(1)} %reshape.401, f32[512]{0:T(512)S(1)} %fusion.50, f32[512]{0:T(512)S(1)} %broadcast_multiply_fusion), kind=kOutput, calls=%fused_computation.12 | convolution fusion | flops 2420244480 | bytes 9447424 | tf_op jit(solution)/shard_map/dot_general | solution.py:30
  307.6 4.1 convolution_convert_fusion.2
  311.8 2.8 fusion.57
  315.9 2.5 convert_reduce_fusion.3
  318.4 6.6 %reshape.388 = bf16[2,2,2,2,2,72,2,384]{7,6,5,4,3,2,1,0:T(2,128)(2,1)S(1)} reshape(bf16[768,2304]{1,0:T(8,128)(2,1)} %convolution_convert_fusion.2) | data formatting | bytes 7077888 | tf_op jit(solution)/shard_map/reshape | solution.py:285
  325.1 9.5 %fusion.62 = (bf16[2,2,2,2,2,72,1,384]{7,6,5,4,3,2,1,0:T(2,128)(2,1)}, bf16[2,2,2,2,2,72,1,384]{7,6,5,4,3,2,1,0:T(2,128)(2,1)}) fusion(bf16[2,2,2,2,2,72,2,384]{7,6,5,4,3,2,1,0:T(2,128)(2,1)S(1)} %reshape.388), kind=kLoop, calls=%fused_computation.243 | loop fusion | bytes 7077888 | tf_op jit(solution)/shard_map/slice | solution.py:290
  334.5 5.8 %constant_dynamic-slice_fusion.4 = (bf16[2,1,2,2,2,72,1,384]{7,6,5,4,3,2,1,0:T(2,128)(2,1)S(1)}, bf16[2,1,2,2,2,72,1,384]{7,6,5,4,3,2,1,0:T(2,128)(2,1)S(1)}) fusion(bf16[2,2,2,2,2,72,1,384]{7,6,5,4,3,2,1,0:T(2,128)(2,1)} %get-tuple-element.45, s32[]{:T(128)S(6)} %select_n.425, s32[]{:T(128)S(6)} %select_n.426), kind=kLoop, calls=%fused_computation.198 | loop fusion | bytes 3538952 | tf_op jit(solution)/shard_map/jit(dynamic_index_in_dim)/dynamic_slice | solution.py:298
  342.2 3.8 constant_dynamic-slice_fusion.6
  359.1 8.5 %squeeze_reshape.10 = bf16[2,2,2,2,2,96,768]{6,5,4,3,2,1,0:T(8,128)(2,1)} reshape(bf16[768,3072]{1,0:T(8,128)(2,1)} %convolution_convert_fusion.1) | data formatting | bytes 9437184 | tf_op jit(solution)/shard_map/squeeze;reshape | solution.py:290
  372.5 9.7 %add_add_fusion.3 = f32[512,768]{1,0:T(8,128)} fusion(f32[512,768]{1,0:T(8,128)} %get-tuple-element.114, bf16[3072,768]{1,0:T(8,128)(2,1)} %all-gather.13.cloned.1.call-done, f32[768]{0:T(1024)S(1)} %copy-done.20, f32[512,3072]{1,0:T(8,128)} %fusion.56, f32[3072]{0:T(1024)S(1)} %copy-done.19), kind=kOutput, calls=%fused_computation.60 | convolution fusion | flops 2432434176 | bytes 14171136 | tf_op jit(solution)/shard_map/dot_general | solution.py:30
  383.8 4.4 convolution_convert_fusion
  388.2 5.4 collective-permute-start.19
  395.5 3.0 collective-permute-start.20
  401.8 7.7 %collective-permute-done.22 = bf16[2,2,2,24,768]{4,3,2,1,0:T(8,128)(2,1)S(1)} collective-permute-done((bf16[2,2,2,24,768]{4,3,2,1,0:T(8,128)(2,1)S(1)}, bf16[2,2,2,24,768]{4,3,2,1,0:T(8,128)(2,1)S(1)}, u32[]{:S(2)}, u32[]{:S(2)}) %collective-permute-start.22) | collective-permute-done | bytes 294944 | tf_op jit(solution)/shard_map/ppermute | solution.py:267
  411.5 3.3 collective-permute-done.23
  419.4 3.2 collective-permute-start.25
  424.8 3.0 collective-permute-start.26
  429.8 2.5 collective-permute-start.27
  436.6 4.5 collective-permute-done.1
  444.0 3.3 collective-permute-done.2
  448.5 3.3 collective-permute-start.12
  452.3 3.8 collective-permute-start.4
  458.8 2.5 collective-permute-start.5
  472.6 26.1 %collective-permute-done.15 = bf16[2,2,72,384]{3,2,0,1:T(8,128)(2,1)S(1)} collective-permute-done((bf16[2,2,72,384]{3,2,0,1:T(8,128)(2,1)S(1)}, bf16[2,2,72,384]{3,2,0,1:T(8,128)(2,1)S(1)}, u32[]{:S(2)}, u32[]{:S(2)}) %collective-permute-start.15) | collective-permute-done | bytes 221216 | tf_op jit(solution)/shard_map/ppermute | solution.py:267
  501.5 7.7 %collective-permute-done.31 = bf16[2,2,96,768]{3,2,1,0:T(8,128)(2,1)S(1)} collective-permute-done((bf16[2,2,96,768]{3,2,1,0:T(8,128)(2,1)S(1)}, bf16[2,2,96,768]{3,2,1,0:T(8,128)(2,1)S(1)}, u32[]{:S(2)}, u32[]{:S(2)}) %collective-permute-start.31) | collective-permute-done | bytes 589856 | tf_op jit(solution)/shard_map/ppermute | solution.py:267
  512.2 7.1 %collective-permute-done.32 = bf16[2,96,768]{2,1,0:T(8,128)(2,1)S(1)} collective-permute-done((bf16[2,96,768]{2,1,0:T(8,128)(2,1)S(1)}, bf16[2,96,768]{2,1,0:T(8,128)(2,1)S(1)}, u32[]{:S(2)}, u32[]{:S(2)}) %collective-permute-start.32) | collective-permute-done | bytes 294944 | tf_op jit(solution)/shard_map/ppermute | solution.py:267
  520.7 6.4 %collective-permute-done.40 = bf16[2,96,768]{2,1,0:T(8,128)(2,1)S(1)} collective-permute-done((bf16[2,96,768]{2,1,0:T(8,128)(2,1)S(1)}, bf16[2,96,768]{2,1,0:T(8,128)(2,1)S(1)}, u32[]{:S(2)}, u32[]{:S(2)}) %collective-permute-start.40) | collective-permute-done | bytes 294944 | tf_op jit(solution)/shard_map/ppermute | solution.py:267
  530.4 5.9 %collective-permute-done.41 = bf16[96,768]{1,0:T(8,128)(2,1)S(1)} collective-permute-done((bf16[96,768]{1,0:T(8,128)(2,1)S(1)}, bf16[96,768]{1,0:T(8,128)(2,1)S(1)}, u32[]{:S(2)}, u32[]{:S(2)}) %collective-permute-start.41) | collective-permute-done | bytes 147488 | tf_op jit(solution)/shard_map/ppermute | solution.py:267
  539.0 4.1 collective-permute-done.42
  543.3 2.9 collective-permute-done.35
  553.5 2.6 reshape.415
  559.4 4.3 collective-permute-done.44
  (316 shorter events, 127.5 us)
Async XLA Ops:
  7.3 35.9 %all-gather.7.cloned.1.call-start = ((), (), s32[]{:S(2)}) async-start(), calls=%async_computation | async-start | bytes 4423680 | tf_op jit(solution)/shard_map/all_gather | solution.py:353
  8.0 147.4 %all-gather.9.cloned.1.call-start = ((), (), s32[]{:S(2)}) async-start(), calls=%async_computation.1 | async-start | bytes 1474560 | tf_op jit(solution)/shard_map/all_gather | solution.py:354
  8.8 152.0 %all-gather.11.cloned.1.call-start = ((), (), s32[]{:S(2)}) async-start(), calls=%async_computation.2 | async-start | bytes 5898240 | tf_op jit(solution)/shard_map/all_gather | solution.py:355
  9.5 167.8 %all-gather.13.cloned.1.call-start = ((), (), s32[]{:S(2)}) async-start(), calls=%async_computation.3 | async-start | bytes 5898240 | tf_op jit(solution)/shard_map/all_gather | solution.py:356
  341.4 75.1 %collective-permute-start.8 = (bf16[2,2,2,2,72,384]{5,4,3,2,1,0:T(8,128)(2,1)}, bf16[2,2,2,2,72,384]{5,4,3,2,1,0:T(8,128)(2,1)}, u32[]{:S(2)}, u32[]{:S(2)}) collective-permute-start(bf16[2,2,2,2,72,384]{5,4,3,2,1,0:T(8,128)(2,1)} %bitcast.271), channel_id=1, source_target_pairs={{0,1},{1,0},{2,3},{3,2},{4,5},{5,4},{6,7},{7,6},{8,9},{9,8},{10,11... | collective-permute-start | bytes 2654216 | tf_op jit(solution)/shard_map/ppermute | solution.py:267
  347.2 80.7 %collective-permute-start = (bf16[2,2,2,2,72,384]{5,4,1,2,3,0:T(8,128)(2,1)}, bf16[2,2,2,2,72,384]{5,4,1,2,3,0:T(8,128)(2,1)}, u32[]{:S(2)}, u32[]{:S(2)}) collective-permute-start(bf16[2,2,2,2,72,384]{5,4,1,2,3,0:T(8,128)(2,1)} %bitcast.272), channel_id=1, source_target_pairs={{0,1},{1,0},{2,3},{3,2},{4,5},{5,4},{6,7},{7,6},{8,9},{9,8},{10,11... | collective-permute-start | bytes 2654216 | tf_op jit(solution)/shard_map/ppermute | solution.py:267
  356.7 13.3 %collective-permute-start.16 = (f32[4,2304]{1,0:T(4,128)}, f32[4,2304]{1,0:T(4,128)}, u32[]{:S(2)}, u32[]{:S(2)}) collective-permute-start(f32[4,2304]{1,0:T(4,128)} %concatenate.27), channel_id=1, source_target_pairs={{0,1},{1,0},{2,3},{3,2},{4,5},{5,4},{6,7},{7,6},{8,9},{9,8},{10,11... | collective-permute-start | bytes 110600 | tf_op jit(solution)/shard_map/ppermute | solution.py:267
  359.1 36.4 %collective-permute-start.21 = (bf16[2,2,2,2,24,768]{5,4,3,2,1,0:T(8,128)(2,1)}, bf16[2,2,2,2,24,768]{5,4,3,2,1,0:T(8,128)(2,1)}, u32[]{:S(2)}, u32[]{:S(2)}) collective-permute-start(bf16[2,2,2,2,24,768]{5,4,3,2,1,0:T(8,128)(2,1)} %dynamic-slice_bitcast_fusion.5), channel_id=1, source_target_pairs={{0,1},{1,0},{2,3},{3,2},{4,5},{5,4},{6,7},{7,6},{8,9},{9,8},{10,11... | collective-permute-start | bytes 1769480 | tf_op jit(solution)/shard_map/ppermute | solution.py:267
  369.5 97.2 %collective-permute-start.29 = (bf16[2,2,2,2,96,768]{5,4,3,2,1,0:T(8,128)(2,1)S(1)}, bf16[2,2,2,2,96,768]{5,4,3,2,1,0:T(8,128)(2,1)S(1)}, u32[]{:S(2)}, u32[]{:S(2)}) collective-permute-start(bf16[2,2,2,2,96,768]{5,4,3,2,1,0:T(8,128)(2,1)S(1)} %dynamic-slice_bitcast_fusion), channel_id=1, source_target_pairs={{0,1},{1,0},{2,3},{3,2},{4,5},{5,4},{6,7},{7,6},{8,9},{9,8},{10,11... | collective-permute-start | bytes 7077896 | tf_op jit(solution)/shard_map/ppermute | solution.py:267
  371.0 11.2 %collective-permute-start.17 = (f32[4,2304]{1,0:T(4,128)S(1)}, f32[4,2304]{1,0:T(4,128)S(1)}, u32[]{:S(2)}, u32[]{:S(2)}) collective-permute-start(f32[4,2304]{1,0:T(4,128)S(1)} %add.385), channel_id=1, source_target_pairs={{0,2},{1,3},{2,0},{3,1},{4,6},{5,7},{6,4},{7,5},{8,10},{9,11},{10,... | collective-permute-start | bytes 110600 | tf_op jit(solution)/shard_map/ppermute | solution.py:267
  382.3 5.9 %collective-permute-start.18 = (f32[4,2304]{1,0:T(4,128)S(1)}, f32[4,2304]{1,0:T(4,128)S(1)}, u32[]{:S(2)}, u32[]{:S(2)}) collective-permute-start(f32[4,2304]{1,0:T(4,128)S(1)} %add.386), channel_id=1, source_target_pairs={{0,4},{1,5},{2,6},{3,7},{4,0},{5,1},{6,2},{7,3},{8,12},{9,13},{10,... | collective-permute-start | bytes 110600 | tf_op jit(solution)/shard_map/ppermute | solution.py:267
  388.2 7.3 %collective-permute-start.19 = (f32[4,2304]{1,0:T(4,128)S(1)}, f32[4,2304]{1,0:T(4,128)S(1)}, u32[]{:S(2)}, u32[]{:S(2)}) collective-permute-start(f32[4,2304]{1,0:T(4,128)S(1)} %add.387), channel_id=1, source_target_pairs={{0,8},{1,9},{2,10},{3,11},{4,12},{5,13},{6,14},{7,15},{8,0},{9,1},... | collective-permute-start | bytes 110600 | tf_op jit(solution)/shard_map/ppermute | solution.py:267
  395.5 72.8 %collective-permute-start.37 = (bf16[2,2,2,2,96,768]{5,4,1,2,3,0:T(8,128)(2,1)S(1)}, bf16[2,2,2,2,96,768]{5,4,1,2,3,0:T(8,128)(2,1)S(1)}, u32[]{:S(2)}, u32[]{:S(2)}) collective-permute-start(bf16[2,2,2,2,96,768]{5,4,1,2,3,0:T(8,128)(2,1)S(1)} %bitcast.285), channel_id=1, source_target_pairs={{0,1},{1,0},{2,3},{3,2},{4,5},{5,4},{6,7},{7,6},{8,9},{9,8},{10,11... | collective-permute-start | bytes 7077896 | tf_op jit(solution)/shard_map/ppermute | solution.py:267
  395.5 5.2 collective-permute-start.20
  400.7 8.8 %collective-permute-start.22 = (bf16[2,2,2,24,768]{4,3,2,1,0:T(8,128)(2,1)S(1)}, bf16[2,2,2,24,768]{4,3,2,1,0:T(8,128)(2,1)S(1)}, u32[]{:S(2)}, u32[]{:S(2)}) collective-permute-start(bf16[2,2,2,24,768]{4,3,2,1,0:T(8,128)(2,1)S(1)} %dynamic-slice_bitcast_fusion.10), channel_id=1, source_target_pairs={{0,2},{1,3},{2,0},{3,1},{4,6},{5,7},{6,4},{7,5},{8,10},{9,11},{10,... | collective-permute-start | bytes 884744 | tf_op jit(solution)/shard_map/ppermute | solution.py:267
  409.6 5.2 collective-permute-start.23
  419.4 5.4 collective-permute-start.25
  422.6 12.6 %collective-permute-start.9 = (bf16[2,2,2,72,384]{4,3,2,1,0:T(8,128)(2,1)S(1)}, bf16[2,2,2,72,384]{4,3,2,1,0:T(8,128)(2,1)S(1)}, u32[]{:S(2)}, u32[]{:S(2)}) collective-permute-start(bf16[2,2,2,72,384]{4,3,2,1,0:T(8,128)(2,1)S(1)} %dynamic-slice_bitcast_fusion.6), channel_id=1, source_target_pairs={{0,4},{1,5},{2,6},{3,7},{4,0},{5,1},{6,2},{7,3},{8,12},{9,13},{10,... | collective-permute-start | bytes 1327112 | tf_op jit(solution)/shard_map/ppermute | solution.py:267
  424.8 4.9 collective-permute-start.26
  429.8 4.8 collective-permute-start.27
  432.3 8.8 %collective-permute-start.1 = (bf16[2,2,2,72,384]{4,3,0,1,2:T(8,128)(2,1)S(1)}, bf16[2,2,2,72,384]{4,3,0,1,2:T(8,128)(2,1)S(1)}, u32[]{:S(2)}, u32[]{:S(2)}) collective-permute-start(bf16[2,2,2,72,384]{4,3,0,1,2:T(8,128)(2,1)S(1)} %dynamic-slice_bitcast_fusion.7), channel_id=1, source_target_pairs={{0,2},{1,3},{2,0},{3,1},{4,6},{5,7},{6,4},{7,5},{8,10},{9,11},{10,... | collective-permute-start | bytes 1327112 | tf_op jit(solution)/shard_map/ppermute | solution.py:267
  434.7 7.3 %collective-permute-start.28 = (bf16[2,2,24,768]{3,2,0,1:T(8,128)(2,1)S(1)}, bf16[2,2,24,768]{3,2,0,1:T(8,128)(2,1)S(1)}, u32[]{:S(2)}, u32[]{:S(2)}) collective-permute-start(bf16[2,2,24,768]{3,2,0,1:T(8,128)(2,1)S(1)} %pad_maximum_fusion.10), channel_id=1, source_target_pairs={{0,4},{1,5},{2,6},{3,7},{4,0},{5,1},{6,2},{7,3},{8,12},{9,13},{10,... | collective-permute-start | bytes 442376 | tf_op jit(solution)/shard_map/ppermute | solution.py:267
  435.5 8.1 %collective-permute-start.10 = (bf16[2,2,72,384]{3,2,1,0:T(8,128)(2,1)S(1)}, bf16[2,2,72,384]{3,2,1,0:T(8,128)(2,1)S(1)}, u32[]{:S(2)}, u32[]{:S(2)}) collective-permute-start(bf16[2,2,72,384]{3,2,1,0:T(8,128)(2,1)S(1)} %dynamic-slice_bitcast_fusion.11), channel_id=1, source_target_pairs={{0,2},{1,3},{2,0},{3,1},{4,6},{5,7},{6,4},{7,5},{8,10},{9,11},{10,... | collective-permute-start | bytes 663560 | tf_op jit(solution)/shard_map/ppermute | solution.py:267
  441.3 6.0 %collective-permute-start.2 = (bf16[2,2,72,384]{3,2,0,1:T(8,128)(2,1)S(1)}, bf16[2,2,72,384]{3,2,0,1:T(8,128)(2,1)S(1)}, u32[]{:S(2)}, u32[]{:S(2)}) collective-permute-start(bf16[2,2,72,384]{3,2,0,1:T(8,128)(2,1)S(1)} %dynamic-slice_bitcast_fusion.12), channel_id=1, source_target_pairs={{0,4},{1,5},{2,6},{3,7},{4,0},{5,1},{6,2},{7,3},{8,12},{9,13},{10,... | collective-permute-start | bytes 663560 | tf_op jit(solution)/shard_map/ppermute | solution.py:267
  443.6 4.8 collective-permute-start.11
  447.4 4.9 collective-permute-start.3
  448.5 7.6 %collective-permute-start.12 = (bf16[72,384]{1,0:T(8,128)(2,1)S(1)}, bf16[72,384]{1,0:T(8,128)(2,1)S(1)}, u32[]{:S(2)}, u32[]{:S(2)}) collective-permute-start(bf16[72,384]{1,0:T(8,128)(2,1)S(1)} %dynamic-slice_bitcast_fusion.19), channel_id=1, source_target_pairs={{0,16},{1,17},{2,18},{3,19},{4,20},{5,21},{6,22},{7,23},{8,24},{9,... | collective-permute-start | bytes 165896 | tf_op jit(solution)/shard_map/ppermute | solution.py:267
  452.3 6.5 %collective-permute-start.4 = (bf16[72,384]{1,0:T(8,128)(2,1)S(1)}, bf16[72,384]{1,0:T(8,128)(2,1)S(1)}, u32[]{:S(2)}, u32[]{:S(2)}) collective-permute-start(bf16[72,384]{1,0:T(8,128)(2,1)S(1)} %dynamic-slice_bitcast_fusion.20), channel_id=1, source_target_pairs={{0,16},{1,17},{2,18},{3,19},{4,20},{5,21},{6,22},{7,23},{8,24},{9,... | collective-permute-start | bytes 165896 | tf_op jit(solution)/shard_map/ppermute | solution.py:267
  456.1 5.6 collective-permute-start.13
  458.8 5.7 collective-permute-start.5
  461.8 4.8 collective-permute-start.14
  464.6 7.2 %collective-permute-start.6 = (bf16[2,72,384]{2,1,0:T(8,128)(2,1)S(1)}, bf16[2,72,384]{2,1,0:T(8,128)(2,1)S(1)}, u32[]{:S(2)}, u32[]{:S(2)}) collective-permute-start(bf16[2,72,384]{2,1,0:T(8,128)(2,1)S(1)} %pad_maximum_fusion.11), channel_id=1, source_target_pairs={{0,8},{1,9},{2,10},{3,11},{4,12},{5,13},{6,14},{7,15},{8,0},{9,1},... | collective-permute-start | bytes 331784 | tf_op jit(solution)/shard_map/ppermute | solution.py:267
  467.6 31.2 %collective-permute-start.30 = (bf16[2,2,2,96,768]{4,3,2,1,0:T(8,128)(2,1)S(1)}, bf16[2,2,2,96,768]{4,3,2,1,0:T(8,128)(2,1)S(1)}, u32[]{:S(2)}, u32[]{:S(2)}) collective-permute-start(bf16[2,2,2,96,768]{4,3,2,1,0:T(8,128)(2,1)S(1)} %dynamic-slice_bitcast_fusion.2), channel_id=1, source_target_pairs={{0,4},{1,5},{2,6},{3,7},{4,0},{5,1},{6,2},{7,3},{8,12},{9,13},{10,... | collective-permute-start | bytes 3538952 | tf_op jit(solution)/shard_map/ppermute | solution.py:267
  469.2 31.2 %collective-permute-start.38 = (bf16[2,2,2,96,768]{4,3,0,1,2:T(8,128)(2,1)S(1)}, bf16[2,2,2,96,768]{4,3,0,1,2:T(8,128)(2,1)S(1)}, u32[]{:S(2)}, u32[]{:S(2)}) collective-permute-start(bf16[2,2,2,96,768]{4,3,0,1,2:T(8,128)(2,1)S(1)} %dynamic-slice_bitcast_fusion.1), channel_id=1, source_target_pairs={{0,2},{1,3},{2,0},{3,1},{4,6},{5,7},{6,4},{7,5},{8,10},{9,11},{10,... | collective-permute-start | bytes 3538952 | tf_op jit(solution)/shard_map/ppermute | solution.py:267
  470.3 28.4 %collective-permute-start.15 = (bf16[2,2,72,384]{3,2,0,1:T(8,128)(2,1)S(1)}, bf16[2,2,72,384]{3,2,0,1:T(8,128)(2,1)S(1)}, u32[]{:S(2)}, u32[]{:S(2)}) collective-permute-start(bf16[2,2,72,384]{3,2,0,1:T(8,128)(2,1)S(1)} %pad_maximum_fusion.9), channel_id=1, source_target_pairs={{0,4},{1,5},{2,6},{3,7},{4,0},{5,1},{6,2},{7,3},{8,12},{9,13},{10,... | collective-permute-start | bytes 663560 | tf_op jit(solution)/shard_map/ppermute | solution.py:267
  471.8 29.5 %collective-permute-start.7 = (bf16[2,2,72,384]{3,2,0,1:T(8,128)(2,1)S(1)}, bf16[2,2,72,384]{3,2,0,1:T(8,128)(2,1)S(1)}, u32[]{:S(2)}, u32[]{:S(2)}) collective-permute-start(bf16[2,2,72,384]{3,2,0,1:T(8,128)(2,1)S(1)} %pad_maximum_fusion.8), channel_id=1, source_target_pairs={{0,4},{1,5},{2,6},{3,7},{4,0},{5,1},{6,2},{7,3},{8,12},{9,13},{10,... | collective-permute-start | bytes 663560 | tf_op jit(solution)/shard_map/ppermute | solution.py:267
  499.2 9.9 %collective-permute-start.31 = (bf16[2,2,96,768]{3,2,1,0:T(8,128)(2,1)S(1)}, bf16[2,2,96,768]{3,2,1,0:T(8,128)(2,1)S(1)}, u32[]{:S(2)}, u32[]{:S(2)}) collective-permute-start(bf16[2,2,96,768]{3,2,1,0:T(8,128)(2,1)S(1)} %dynamic-slice_bitcast_fusion.4), channel_id=1, source_target_pairs={{0,2},{1,3},{2,0},{3,1},{4,6},{5,7},{6,4},{7,5},{8,10},{9,11},{10,... | collective-permute-start | bytes 1769480 | tf_op jit(solution)/shard_map/ppermute | solution.py:267
  500.7 9.9 %collective-permute-start.39 = (bf16[2,2,96,768]{3,2,0,1:T(8,128)(2,1)S(1)}, bf16[2,2,96,768]{3,2,0,1:T(8,128)(2,1)S(1)}, u32[]{:S(2)}, u32[]{:S(2)}) collective-permute-start(bf16[2,2,96,768]{3,2,0,1:T(8,128)(2,1)S(1)} %dynamic-slice_bitcast_fusion.3), channel_id=1, source_target_pairs={{0,4},{1,5},{2,6},{3,7},{4,0},{5,1},{6,2},{7,3},{8,12},{9,13},{10,... | collective-permute-start | bytes 1769480 | tf_op jit(solution)/shard_map/ppermute | solution.py:267
  509.4 9.9 %collective-permute-start.32 = (bf16[2,96,768]{2,1,0:T(8,128)(2,1)S(1)}, bf16[2,96,768]{2,1,0:T(8,128)(2,1)S(1)}, u32[]{:S(2)}, u32[]{:S(2)}) collective-permute-start(bf16[2,96,768]{2,1,0:T(8,128)(2,1)S(1)} %dynamic-slice_bitcast_fusion.9), channel_id=1, source_target_pairs={{0,8},{1,9},{2,10},{3,11},{4,12},{5,13},{6,14},{7,15},{8,0},{9,1},... | collective-permute-start | bytes 884744 | tf_op jit(solution)/shard_map/ppermute | solution.py:267
  510.9 16.3 %collective-permute-start.40 = (bf16[2,96,768]{2,1,0:T(8,128)(2,1)S(1)}, bf16[2,96,768]{2,1,0:T(8,128)(2,1)S(1)}, u32[]{:S(2)}, u32[]{:S(2)}) collective-permute-start(bf16[2,96,768]{2,1,0:T(8,128)(2,1)S(1)} %dynamic-slice_bitcast_fusion.8), channel_id=1, source_target_pairs={{0,8},{1,9},{2,10},{3,11},{4,12},{5,13},{6,14},{7,15},{8,0},{9,1},... | collective-permute-start | bytes 884744 | tf_op jit(solution)/shard_map/ppermute | solution.py:267
  519.4 8.7 %collective-permute-start.33 = (bf16[96,768]{1,0:T(8,128)(2,1)S(1)}, bf16[96,768]{1,0:T(8,128)(2,1)S(1)}, u32[]{:S(2)}, u32[]{:S(2)}) collective-permute-start(bf16[96,768]{1,0:T(8,128)(2,1)S(1)} %dynamic-slice_bitcast_fusion.14), channel_id=1, source_target_pairs={{0,16},{1,17},{2,18},{3,19},{4,20},{5,21},{6,22},{7,23},{8,24},{9,... | collective-permute-start | bytes 442376 | tf_op jit(solution)/shard_map/ppermute | solution.py:267
  527.3 9.0 %collective-permute-start.41 = (bf16[96,768]{1,0:T(8,128)(2,1)S(1)}, bf16[96,768]{1,0:T(8,128)(2,1)S(1)}, u32[]{:S(2)}, u32[]{:S(2)}) collective-permute-start(bf16[96,768]{1,0:T(8,128)(2,1)S(1)} %dynamic-slice_bitcast_fusion.13), channel_id=1, source_target_pairs={{0,16},{1,17},{2,18},{3,19},{4,20},{5,21},{6,22},{7,23},{8,24},{9,... | collective-permute-start | bytes 442376 | tf_op jit(solution)/shard_map/ppermute | solution.py:267
  528.2 9.7 %collective-permute-start.34 = (bf16[96,768]{1,0:T(8,128)(2,1)S(1)}, bf16[96,768]{1,0:T(8,128)(2,1)S(1)}, u32[]{:S(2)}, u32[]{:S(2)}) collective-permute-start(bf16[96,768]{1,0:T(8,128)(2,1)S(1)} %fusion.40), channel_id=1, source_target_pairs={{0,16},{1,17},{2,18},{3,19},{4,20},{5,21},{6,22},{7,23},{8,24},{9,... | collective-permute-start | bytes 442376 | tf_op jit(solution)/shard_map/ppermute | solution.py:267
  536.4 6.8 %collective-permute-start.42 = (bf16[96,768]{1,0:T(8,128)(2,1)S(1)}, bf16[96,768]{1,0:T(8,128)(2,1)S(1)}, u32[]{:S(2)}, u32[]{:S(2)}) collective-permute-start(bf16[96,768]{1,0:T(8,128)(2,1)S(1)} %fusion.39), channel_id=1, source_target_pairs={{0,16},{1,17},{2,18},{3,19},{4,20},{5,21},{6,22},{7,23},{8,24},{9,... | collective-permute-start | bytes 442376 | tf_op jit(solution)/shard_map/ppermute | solution.py:267
  538.0 8.2 %collective-permute-start.35 = (bf16[2,96,768]{2,1,0:T(8,128)(2,1)S(1)}, bf16[2,96,768]{2,1,0:T(8,128)(2,1)S(1)}, u32[]{:S(2)}, u32[]{:S(2)}) collective-permute-start(bf16[2,96,768]{2,1,0:T(8,128)(2,1)S(1)} %pad_maximum_fusion.6), channel_id=1, source_target_pairs={{0,8},{1,9},{2,10},{3,11},{4,12},{5,13},{6,14},{7,15},{8,0},{9,1},... | collective-permute-start | bytes 884744 | tf_op jit(solution)/shard_map/ppermute | solution.py:267
  543.2 6.8 %collective-permute-start.43 = (bf16[2,96,768]{2,1,0:T(8,128)(2,1)S(1)}, bf16[2,96,768]{2,1,0:T(8,128)(2,1)S(1)}, u32[]{:S(2)}, u32[]{:S(2)}) collective-permute-start(bf16[2,96,768]{2,1,0:T(8,128)(2,1)S(1)} %pad_maximum_fusion.7), channel_id=1, source_target_pairs={{0,8},{1,9},{2,10},{3,11},{4,12},{5,13},{6,14},{7,15},{8,0},{9,1},... | collective-permute-start | bytes 884744 | tf_op jit(solution)/shard_map/ppermute | solution.py:267
  547.1 10.1 %collective-permute-start.36 = (bf16[2,2,96,768]{3,2,0,1:T(8,128)(2,1)}, bf16[2,2,96,768]{3,2,0,1:T(8,128)(2,1)S(1)}, u32[]{:S(2)}, u32[]{:S(2)}) collective-permute-start(bf16[2,2,96,768]{3,2,0,1:T(8,128)(2,1)} %pad_maximum_fusion.4), channel_id=1, source_target_pairs={{0,4},{1,5},{2,6},{3,7},{4,0},{5,1},{6,2},{7,3},{8,12},{9,13},{10,... | collective-permute-start | bytes 1769480 | tf_op jit(solution)/shard_map/ppermute | solution.py:267
  550.9 12.7 %collective-permute-start.44 = (bf16[2,2,96,768]{3,2,0,1:T(8,128)(2,1)}, bf16[2,2,96,768]{3,2,0,1:T(8,128)(2,1)}, u32[]{:S(2)}, u32[]{:S(2)}) collective-permute-start(bf16[2,2,96,768]{3,2,0,1:T(8,128)(2,1)} %pad_maximum_fusion.5), channel_id=1, source_target_pairs={{0,4},{1,5},{2,6},{3,7},{4,0},{5,1},{6,2},{7,3},{8,12},{9,13},{10,... | collective-permute-start | bytes 1769480 | tf_op jit(solution)/shard_map/ppermute | solution.py:267
  (40 other events, 401.0 us)
Sparse Core Ops, SparseCore 0:
  9.7 33.4 all-gather.6
  44.7 41.0 all-gather.8
  87.4 42.4 all-gather.10
  131.3 45.9 all-gather.12

commit v3 on v1

--- a/solution.py
+++ b/solution.py
@@ -32,7 +32,8 @@
     )
 
 
-def exchange_kernel(source, target, send_sem, recv_sem, local_sem):
+def exchange_kernel(source, *refs):
+    target, send_sem, recv_sem, local_sem = refs[-4:]
     rep = lax.axis_index("rep")
     shard = lax.axis_index("shard")
     across = GROUP // 4
@@ -71,11 +72,11 @@
         copy.wait()
 
 
-def exchange(blocks, number):
+def exchange(blocks, number, *behind):
     return pl.pallas_call(
         exchange_kernel,
         out_shape=jax.ShapeDtypeStruct(blocks.shape, blocks.dtype),
-        in_specs=[pl.BlockSpec(memory_space=pl.ANY)],
+        in_specs=[pl.BlockSpec(memory_space=pl.ANY)] * (1 + len(behind)),
         out_specs=pl.BlockSpec(memory_space=pl.ANY),
         scratch_shapes=[
             pltpu.SemaphoreType.DMA((GROUP,)),
@@ -84,7 +85,7 @@
         ],
         compiler_params=pltpu.CompilerParams(collective_id=number, has_side_effects=True),
         name="exchange",
-    )(blocks)
+    )(blocks, *behind)
 
 
 def tile_mask(chunk, first_row, last_row):
@@ -174,8 +175,9 @@
 
 def attend_back_kernel(
     heads, size, low_ref, high_ref, first_ref, last_ref, pack_ref, slope_ref, mixed_ref, lse_ref,
-    out_ref, total_ref,
+    *refs,
 ):
+    out_ref, total_ref = refs[-2:]
     step = pl.program_id(0)
     rows = pack_ref.shape[2] - TILE
     half = rows // 2
@@ -230,7 +232,7 @@
             out_ref[block, :, :rows] = total_ref[block].astype(out_ref.dtype)
 
 
-def attend_back(low, high, first, last, pack, slope, mixed, lse, heads, size):
+def attend_back(low, high, first, last, pack, slope, mixed, lse, heads, size, *behind):
     blocks, rows, lanes = pack.shape
     row_spec = pl.BlockSpec((1, 1, TILE), lambda i, *_: (i, 0, 0))
     whole = pl.BlockSpec((blocks, rows, lanes), lambda i, *_: (0, 0, 0))
@@ -248,7 +250,8 @@
                 tile_spec,
                 tile_spec,
                 pl.BlockSpec((1, 8, TILE), lambda i, *_: (i, 0, 0)),
-            ],
+            ]
+            + [pl.BlockSpec(memory_space=pl.ANY)] * len(behind),
             out_specs=whole,
             scratch_shapes=[pltpu.VMEM((blocks, rows, lanes - TILE), jnp.float32)],
         ),
@@ -259,20 +262,74 @@
             transcendentals=heads * TILE * TILE * 40,
         ),
         name="attend_back",
-    )(low, high, first, last, pack, slope, mixed, lse)
-
-
-def reduce_weight(grad):
-    part = lax.psum_scatter(
-        grad.astype(jnp.bfloat16), "shard", scatter_dimension=0, tiled=True
-    )
-    count = lax.axis_size("rep")
-    rows, columns = part.shape
-    part = lax.psum_scatter(
-        part.reshape(count, rows * columns // count // 768, 768), "rep", scatter_dimension=0,
-        tiled=False,
-    )
-    return lax.all_gather(part, "rep", axis=0, tiled=False).reshape(rows, columns)
+    )(low, high, first, last, pack, slope, mixed, lse, *behind)
+
+
+def swap_with(value, bit):
+    count = lax.axis_size(("rep", "shard"))
+    return lax.ppermute(
+        value, ("rep", "shard"), [(index, index ^ (1 << bit)) for index in range(count)]
+    )
+
+
+def bit_of(index, bit):
+    return lax.rem(index // (1 << bit), 2)
+
+
+class WeightSum:
+    def __init__(self, grad, pieces=1, turned=False):
+        count = lax.axis_size(("rep", "shard"))
+        self.bits = count.bit_length() - 1
+        self.shards = lax.axis_size("shard")
+        self.shard_bits = self.shards.bit_length() - 1
+        self.index = lax.axis_index("rep") * self.shards + lax.axis_index("shard")
+        self.shape = grad.shape
+        rows, columns = grad.shape
+        names = list(range(self.shard_bits - 1, -1, -1))
+        names += list(range(self.bits - 1, self.shard_bits - 1, -1))
+        low = grad.astype(jnp.bfloat16)
+        low = low.reshape((2,) * self.bits + (rows * columns // count // 768, pieces, 768 // pieces))
+        self.parts = [low[..., piece, :] for piece in range(pieces)]
+        self.left = [list(names) for _ in range(pieces)]
+        self.orders = []
+        for piece in range(pieces):
+            order = list(range(self.bits))
+            if (piece % 2 == 1) != turned:
+                order[1:3] = order[2:0:-1]
+            self.orders.append(order)
+
+    def halve(self):
+        for piece, part in enumerate(self.parts):
+            bit = self.orders[piece].pop(0)
+            axis = self.left[piece].index(bit)
+            mine = bit_of(self.index, bit)
+            keep = lax.dynamic_index_in_dim(part, mine, axis, keepdims=False)
+            give = lax.dynamic_index_in_dim(part, 1 - mine, axis, keepdims=False)
+            came = swap_with(give, bit)
+            total = keep.astype(jnp.float32) + came.astype(jnp.float32)
+            self.parts[piece] = total.astype(jnp.bfloat16)
+            self.left[piece].remove(bit)
+        return self.parts[0]
+
+    def finish(self):
+        while self.orders[0]:
+            self.halve()
+        for bit in range(self.bits - 1, self.shard_bits - 1, -1):
+            mine = bit_of(self.index, bit)
+            axis = self.bits - 1 - bit
+            for piece, part in enumerate(self.parts):
+                came = swap_with(part, bit)
+                low = jnp.where(mine == 0, part, came)
+                high = jnp.where(mine == 0, came, part)
+                self.parts[piece] = jnp.stack([low, high], axis=axis)
+        whole = jnp.stack(self.parts, axis=-2) if len(self.parts) > 1 else self.parts[0]
+        return whole.reshape(self.shape[0] // self.shards, self.shape[1])
+
+
+def reduce_small(value):
+    for bit in range(lax.axis_size(("rep", "shard")).bit_length() - 1):
+        value = value + swap_with(value, bit)
+    return value
 
 
 def body(
@@ -368,25 +425,32 @@
     active_low = active.astype(bf16)
     layer_out = middle + dot(active_low, full_wdown, 1, 0) + down_bias
     grad_out = cotangent.astype(f32)
-    grad_wdown = reduce_weight(dot(active_low, cotangent, 0, 0))
+    sum_wdown = WeightSum(dot(active_low, cotangent, 0, 0))
+    down_core = sum_wdown.halve()
     grad_down_bias = jnp.sum(grad_out, axis=0)
     (grad_hidden,) = gelu_back(dot(cotangent, full_wdown, 1, 1))
     hidden_low = grad_hidden.astype(bf16)
-    grad_wup = reduce_weight(dot(second_low, hidden_low, 0, 0))
+    sum_wup = WeightSum(dot(second_low, hidden_low, 0, 0), 1, True)
+    up_start = sum_wup.parts[0]
+    up_core = sum_wup.halve()
     grad_up_bias = jnp.sum(hidden_low.astype(f32), axis=0)
     grad_second = dot(hidden_low, full_wup, 1, 1)
     grad_middle_norm, grad_gain_two, grad_offset_two = norm_two_back(grad_second)
     grad_middle = grad_out + grad_middle_norm
     middle_low = grad_middle.astype(bf16)
-    grad_wout = reduce_weight(dot(mixed_low, middle_low, 1, 0))
+    sum_wout = WeightSum(dot(mixed_low, middle_low, 1, 0))
+    out_core = sum_wout.halve()
     grad_out_bias = jnp.sum(middle_low.astype(f32), axis=0)
     grad_mixed = dot(full_wout, middle_low, 1, 1).astype(bf16)
 
     slope = exchange(
-        by_side(grad_mixed.reshape(shards, part, tok_rows)).reshape(GROUP, part, TILE), 3
-    )
-    grad_pack = attend_back(low, high, first, last, pack, slope, mixed_tiles, lse, heads, size)
-    returned = exchange(grad_pack, 4).reshape(halves, shards, part, 2 * tok_rows + TILE)
+        by_side(grad_mixed.reshape(shards, part, tok_rows)).reshape(GROUP, part, TILE), 3,
+        down_core, up_start,
+    )
+    grad_pack = attend_back(low, high, first, last, pack, slope, mixed_tiles, lse, heads, size, up_core, out_core)
+    returned = exchange(
+        grad_pack, 4, sum_wdown.halve(), sum_wup.halve(), sum_wout.halve()
+    ).reshape(halves, shards, part, 2 * tok_rows + TILE)
     grad_pairs = jnp.sum(returned[..., : 2 * tok_rows].astype(f32), axis=0).astype(bf16)
     grad_projected = jnp.stack(
         [
@@ -396,7 +460,8 @@
         ],
         axis=0,
     ).reshape(3 * width, tok_rows)
-    grad_wqkv = reduce_weight(dot(normed_low, grad_projected, 0, 1))
+    grad_wqkv = WeightSum(dot(normed_low, grad_projected, 0, 1), 2).finish()
+    grad_wdown, grad_wup, grad_wout = sum_wdown.finish(), sum_wup.finish(), sum_wout.finish()
     bias_grads = jnp.sum(grad_projected.astype(f32), axis=1)
     grad_query_bias = bias_grads[:width]
     grad_value_bias = bias_grads[2 * width :]
@@ -410,7 +475,7 @@
     )
     laid = jnp.concatenate([value.reshape(shards, -1) for value in small_grads], axis=1)
     summed = lax.dynamic_index_in_dim(
-        lax.psum(laid, ("rep", "shard")), shard, 0, keepdims=False
+        reduce_small(laid), shard, 0, keepdims=False
     )
     pieces = []
     at = 0

time: 773 us -> 556 us (0.72)
  waiting for transfers between devices: 308 us -> 110 us
  blocking collectives: 111 us -> 6.2 us
  local copies, waits for them, and re-layouts: 32.7 us -> 86.1 us
  starting transfers between devices: 0.94 us -> 45.5 us
  matrix products: 68.7 us -> 53.2 us
  other arithmetic: 25.1 us -> 36.9 us
  Pallas kernels: 207 us -> 197 us
    reduce_scatter x8 -> x0, waiting for transfers between devices: 226 us -> none  [the longest x4 165 us: reduce_weight(): lax.psum_scatter(part.reshape(count, rows * columns // count // 768, 768)...]
    ppermute x0 -> x45, waiting for transfers between devices: none -> 76.6 us  [swap_with(): lax.ppermute(value, ('rep', 'shard'), [(index, index ^ 1 << bit) for inde...]
    all_gather x2 -> x0, blocking collectives: 64.2 us -> none  [reduce_weight(): lax.all_gather(part, 'rep', axis=0, tiled=False).reshape(rows, columns)]
    all_gather x2 -> x0, waiting for transfers between devices: 49.5 us -> none  [reduce_weight(): lax.all_gather(part, 'rep', axis=0, tiled=False).reshape(rows, columns)]
    ppermute x0 -> x45, starting transfers between devices: none -> 45.3 us  [swap_with(): lax.ppermute(value, ('rep', 'shard'), [(index, index ^ 1 << bit) for inde...]
    psum x1 -> x0, blocking collectives: 40.6 us -> none  [body(): lax.psum(laid, ('rep', 'shard'))]
    dynamic_slice x0 -> x5, local copies, waits for them, and re-layouts: none -> 18.1 us  [the longest x3 14.9 us: halve(): keep = lax.dynamic_index_in_dim(part, mine, axis, keepdims=False)]
    dot_general x12, matrix products: 68.7 us -> 53.2 us  [dot(): lax.dot_general(left, right, (((left_dim,), (right_dim,)), ((), ())), pre...]
  transfers between devices with their start and end apart: 14 -> 49, of which waited for: 10 -> 22; matrix products, arithmetic and copies ran while one was open for 12% -> 22% of each run, Pallas kernels for 27% -> 27%
where the time goes in v3:
time: 556 us; the launch traced here: 550 us
  Pallas kernels  197 us (35%)
  waiting for transfers between devices  110 us (20%)
  local copies, waits for them, and re-layouts  86.1 us (15%)
  matrix products  53.2 us (10%)
  starting transfers between devices  45.5 us (8%)
  other arithmetic  36.9 us (7%)
  between operations  16.2 us (3%)
  blocking collectives  6.2 us (1%)
    pallas_call x4, Pallas kernels, exchange(): pl.pallas_call(exchange_kernel, out_shape=jax.ShapeDtypeStruct(blocks.sha...  139 us
    ppermute x45, waiting for transfers between devices, swap_with(): lax.ppermute(value, ('rep', 'shard'), [(index, index ^ 1 << bit) for inde...  76.6 us
    dot_general x12, matrix products, dot(): lax.dot_general(left, right, (((left_dim,), (right_dim,)), ((), ())), pre...  53.2 us
    ppermute x45, starting transfers between devices, swap_with(): lax.ppermute(value, ('rep', 'shard'), [(index, index ^ 1 << bit) for inde...  45.3 us
    pallas_call x1, Pallas kernels, attend_back(): pl.pallas_call(functools.partial(attend_back_kernel, heads, size), out_sh...  28.7 us
    pallas_call x1, Pallas kernels, attend(): pl.pallas_call(functools.partial(attend_kernel, heads, size), out_shape=(...  28.6 us
    unnamed x130, local copies, waits for them, and re-layouts  19.6 us
    all_gather x1, waiting for transfers between devices, body(): full_qkv = lax.all_gather(w_qkv, 'shard', axis=0, tiled=True)  18.6 us
  transfers between devices with their start and end apart: 49, of which 22 were waited for; matrix products, arithmetic and copies ran while one was open for 22% of the time, Pallas kernels for 27%

profile of v3, /device:TPU:0, one launch (start us, length us, event | category | flops | bytes accessed | tf_op | source)
XLA Modules:
  0.0 550.2 jit_solution(16251917327850865062)
XLA Ops:
  10.4 6.2 %all-gather.1 = bf16[4,1,2304]{2,1,0:T(2,128)(2,1)S(1)} all-gather(bf16[1,1,2304]{2,1,0:T(2,128)(2,1)S(1)} %reshape.435), channel_id=2, replica_groups=mesh['rep'=8,'shard'=4] {'shard'}, dimensions={0}, use_global_device_ids=true | all-gather | bytes 23040 | tf_op jit(solution)/shard_map/all_gather | solution.py:358
  18.1 2.7 convert_reduce_fusion.5
  24.6 18.6 %all-gather.7.cloned.1.call-done = bf16[768,2304]{1,0:T(8,128)(2,1)} async-done(((bf16[192,2304]{1,0:T(8,128)(2,1)}), bf16[768,2304]{1,0:T(8,128)(2,1)}) %all-gather.7.cloned.1.call-update) | async-done | bytes 3538960 | tf_op jit(solution)/shard_map/all_gather | solution.py:367
  43.2 4.2 fusion.10
  50.9 2.6 maximum_maximum_fusion
  53.5 50.4 %exchange.4.pack_ref = bf16[8,192,1280]{2,1,0:T(8,128)(2,1)} custom-call(bf16[8,192,1280]{2,1,0:T(8,128)(2,1)} %bitcast.281), custom_call_target="tpu_custom_call" | custom-call | tf_op jit(solution)/shard_map/exchange/pallas_call | solution.py:76
  106.0 28.6 %attend.1 = (f32[8,192,256]{2,1,0:T(8,128)S(1)}, f32[8,8,256]{2,1,0:T(8,128)S(1)}) custom-call(s32[8]{0:T(128)S(1)} %and_select_fusion.low_ref, s32[8]{0:T(128)S(1)} %get-tuple-element.37.high_ref, s32[8,1,256]{2,1,0:T(1,128)S(1)} %get-tuple-element.114.first_ref, s32[8,1,256]{2,1,0:T(1,128)S(1)} %get-tuple-element.113.last_ref, ...), custom_call_target="tpu_custom_call" | custom-call | flops 2013265920 | bytes 3932160 | tf_op jit(solution)/shard_map/attend/pallas_call | solution.py:147
  136.7 17.9 %exchange.5 = bf16[8,192,256]{2,1,0:T(8,128)(2,1)} custom-call(bf16[8,192,256]{2,1,0:T(8,128)(2,1)} %convert_element_type.486.source), custom_call_target="tpu_custom_call" | custom-call | tf_op jit(solution)/shard_map/exchange/pallas_call | solution.py:76
  155.8 2.2 fusion.66
  158.4 7.1 %fusion.56 = f32[512,3072]{1,0:T(8,128)} fusion(bf16[768,3072]{1,0:T(8,128)(2,1)} %all-gather.11.cloned.1.call-done, f32[512,768]{1,0:T(8,128)S(1)} %get-tuple-element.116, f32[768]{0:T(1024)S(1)} %reshape.402, f32[768]{0:T(1024)S(1)} %reshape.401, f32[512]{0:T(512)S(1)} %fusion.50, f32[512]{0:T(512)S(1)} %broadcast_multiply_fusion), kind=kOutput, calls=%fused_computation.243 | convolution fusion | flops 2417885184 | bytes 12593152 | tf_op jit(solution)/shard_map/dot_general | solution.py:30
  165.5 11.7 %all-gather.13.cloned.1.call-done = bf16[3072,768]{1,0:T(8,128)(2,1)} async-done(((bf16[768,768]{1,0:T(8,128)(2,1)}), bf16[3072,768]{1,0:T(8,128)(2,1)}) %all-gather.13.cloned.1.call-update) | async-done | bytes 4718608 | tf_op jit(solution)/shard_map/all_gather | solution.py:370
  177.2 9.7 %convert_reduce_fusion = (f32[3072]{0:T(1024)}, bf16[512,3072]{1,0:T(8,128)(2,1)S(1)}) fusion(f32[512,3072]{1,0:T(8,128)} %fusion.56, f32[3072]{0:T(1024)S(1)} %reshape.403, bf16[512,768]{1,0:T(8,128)(2,1)S(1)} %copy-done.21, bf16[3072,768]{1,0:T(8,128)(2,1)} %all-gather.13.cloned.1.call-done), kind=kOutput, calls=%fused_computation.9 | convolution fusion | flops 2452091904 | bytes 14966784 | tf_op jit(solution)/shard_map/dot_general | solution.py:30
  187.0 3.5 multiply_reduce_fusion
  194.2 4.3 convolution_convert_fusion.2
  199.1 4.9 convolution_convert_fusion.1
  204.0 3.9 collective-permute-done.5
  212.9 8.5 %squeeze_reshape.10.refs_1_ = bf16[2,2,2,2,2,96,768]{6,5,4,3,2,1,0:T(8,128)(2,1)} reshape(bf16[768,3072]{1,0:T(8,128)(2,1)} %convolution_convert_fusion.1) | data formatting | bytes 9437184 | tf_op jit(solution)/shard_map/squeeze;reshape | solution.py:292
  223.0 4.1 constant_dynamic-slice_fusion.6
  229.0 2.5 collective-permute-start.29
  231.5 9.3 %add_add_fusion.3 = f32[512,768]{1,0:T(8,128)} fusion(f32[512,768]{1,0:T(8,128)S(1)} %get-tuple-element.116, bf16[3072,768]{1,0:T(8,128)(2,1)} %all-gather.13.cloned.1.call-done, f32[768]{0:T(1024)S(1)} %copy-done.46, f32[512,3072]{1,0:T(8,128)} %fusion.56, f32[3072]{0:T(1024)S(1)} %copy-done.42), kind=kOutput, calls=%fused_computation.61 | convolution fusion | flops 2432434176 | bytes 14171136 | tf_op jit(solution)/shard_map/dot_general | solution.py:30
  242.5 3.6 collective-permute-done.30
  246.4 4.1 collective-permute-done.31
  251.2 2.3 fusion.8
  256.5 2.3 fusion.7
  268.3 25.1 %exchange.6.slope_ref = bf16[8,192,256]{2,1,0:T(8,128)(2,1)} custom-call(bf16[8,192,256]{2,1,0:T(8,128)(2,1)} %bitcast.283, bf16[2,2,2,2,96,768]{5,4,3,2,1,0:T(8,128)(2,1)} %copy.81.refs_0_, bf16[2,2,2,2,2,96,768]{6,5,4,3,2,1,0:T(8,128)(2,1)} %squeeze_reshape.10.refs_1_), custom_call_target="tpu_custom_call" | custom-call | tf_op jit(solution)/shard_map/exchange/pallas_call | solution.py:76
  298.0 28.7 %attend_back.1.source = bf16[8,192,1280]{2,1,0:T(8,128)(2,1)S(1)} custom-call(s32[8]{0:T(128)S(1)} %and_select_fusion.low_ref, s32[8]{0:T(128)S(1)} %get-tuple-element.37.high_ref, s32[8,1,256]{2,1,0:T(1,128)S(1)} %get-tuple-element.114.first_ref, s32[8,1,256]{2,1,0:T(1,128)S(1)} %get-tuple-element.113.last_ref, bf16[8,192,1280]{2,1,0:T(8,128)(2,1)S(1)} %copy-done.1, ...), custom_call_target="tpu_custom_call" | custom-call | flops 5033164800 | bytes 7864320 | tf_op jit(solution)/shard_map/attend_back/pallas_call | solution.py:240
  333.4 2.6 fusion.15.refs_1_
  336.0 45.9 %exchange.7 = bf16[8,192,1280]{2,1,0:T(8,128)(2,1)} custom-call(bf16[8,192,1280]{2,1,0:T(8,128)(2,1)} %copy-done.2, bf16[2,2,2,96,768]{4,3,2,1,0:T(8,128)(2,1)} %copy.86.refs_0_, bf16[2,2,2,96,768]{4,3,2,1,0:T(8,128)(2,1)} %fusion.15.refs_1_, bf16[2,2,2,24,768]{4,3,2,1,0:T(8,128)(2,1)} %copy-done.23), custom_call_target="tpu_custom_call" | custom-call | tf_op jit(solution)/shard_map/exchange/pallas_call | solution.py:76
  382.0 2.7 slice_reduce_fusion
  388.3 2.3 fusion.57
  395.9 4.1 convolution_convert_fusion
  400.1 6.9 %reshape.388 = bf16[2,2,2,2,2,72,2,384]{7,6,5,4,3,2,1,0:T(2,128)(2,1)S(1)} reshape(bf16[768,2304]{1,0:T(8,128)(2,1)} %convolution_convert_fusion) | data formatting | bytes 7077888 | tf_op jit(solution)/shard_map/reshape | solution.py:291
  409.9 9.5 %fusion.62 = (bf16[2,2,2,2,2,72,1,384]{7,6,5,4,3,2,1,0:T(2,128)(2,1)}, bf16[2,2,2,2,2,72,1,384]{7,6,5,4,3,2,1,0:T(2,128)(2,1)}) fusion(bf16[2,2,2,2,2,72,2,384]{7,6,5,4,3,2,1,0:T(2,128)(2,1)S(1)} %reshape.388), kind=kLoop, calls=%fused_computation.246 | loop fusion | bytes 7077888 | tf_op jit(solution)/shard_map/slice | solution.py:292
  421.7 9.1 %constant_dynamic-slice_fusion.2 = (bf16[2,1,2,2,2,72,1,384]{7,6,5,4,3,2,1,0:T(2,128)(2,1)S(1)}, bf16[2,1,2,2,2,72,1,384]{7,6,5,4,3,2,1,0:T(2,128)(2,1)S(1)}, bf...) fusion(bf16[2,2,2,2,2,72,1,384]{7,6,5,4,3,2,1,0:T(2,128)(2,1)} %get-tuple-element.47, ...), kind=kLoop, calls=%fused_computation.197 | loop fusion | bytes 7077896 | tf_op jit(solution)/shard_map/jit(dynamic_index_in_dim)/dynamic_slice | solution.py:306
  430.8 4.2 collective-permute-start.25
  443.1 12.3 %collective-permute-done.33 = bf16[2,2,96,768]{3,2,1,0:T(8,128)(2,1)S(1)} collective-permute-done((bf16[2,2,96,768]{3,2,1,0:T(8,128)(2,1)S(1)}, bf16[2,2,96,768]{3,2,1,0:T(8,128)(2,1)S(1)}, u32[]{:S(2)}, u32[]{:S(2)}) %collective-permute-start.33) | collective-permute-done | bytes 589856 | tf_op jit(solution)/shard_map/ppermute | solution.py:270
  459.7 5.8 %collective-permute-done.34 = bf16[2,96,768]{2,1,0:T(8,128)(2,1)S(1)} collective-permute-done((bf16[2,96,768]{2,1,0:T(8,128)(2,1)S(1)}, bf16[2,96,768]{2,1,0:T(8,128)(2,1)S(1)}, u32[]{:S(2)}, u32[]{:S(2)}) %collective-permute-start.34) | collective-permute-done | bytes 294944 | tf_op jit(solution)/shard_map/ppermute | solution.py:270
  466.6 6.2 %collective-permute-done.40 = bf16[2,96,768]{2,1,0:T(8,128)(2,1)S(1)} collective-permute-done((bf16[2,96,768]{2,1,0:T(8,128)(2,1)S(1)}, bf16[2,96,768]{2,1,0:T(8,128)(2,1)S(1)}, u32[]{:S(2)}, u32[]{:S(2)}) %collective-permute-start.40) | collective-permute-done | bytes 294944 | tf_op jit(solution)/shard_map/ppermute | solution.py:270
  473.1 6.5 %collective-permute-done.35 = bf16[96,768]{1,0:T(8,128)(2,1)S(1)} collective-permute-done((bf16[96,768]{1,0:T(8,128)(2,1)S(1)}, bf16[96,768]{1,0:T(8,128)(2,1)S(1)}, u32[]{:S(2)}, u32[]{:S(2)}) %collective-permute-start.35) | collective-permute-done | bytes 147488 | tf_op jit(solution)/shard_map/ppermute | solution.py:270
  479.7 3.0 collective-permute-done.41
  482.9 8.4 %collective-permute-done.36 = bf16[96,768]{1,0:T(8,128)(2,1)S(1)} collective-permute-done((bf16[96,768]{1,0:T(8,128)(2,1)S(1)}, bf16[96,768]{1,0:T(8,128)(2,1)S(1)}, u32[]{:S(2)}, u32[]{:S(2)}) %collective-permute-start.36) | collective-permute-done | bytes 147488 | tf_op jit(solution)/shard_map/ppermute | solution.py:270
  495.8 5.6 %collective-permute-done.37 = bf16[2,96,768]{2,1,0:T(8,128)(2,1)S(1)} collective-permute-done((bf16[2,96,768]{2,1,0:T(8,128)(2,1)S(1)}, bf16[2,96,768]{2,1,0:T(8,128)(2,1)S(1)}, u32[]{:S(2)}, u32[]{:S(2)}) %collective-permute-start.37) | collective-permute-done | bytes 294944 | tf_op jit(solution)/shard_map/ppermute | solution.py:270
  501.6 4.4 collective-permute-done.43
  508.6 2.6 collective-permute-done.17
  511.2 2.2 collective-permute-start.18
  522.3 3.3 collective-permute-start.20
  525.6 2.5 collective-permute-start.12
  540.9 2.6 reshape.421
  (367 shorter events, 112.4 us)
Async XLA Ops:
  7.3 35.9 %all-gather.7.cloned.1.call-start = ((), (), s32[]{:S(2)}) async-start(), calls=%async_computation | async-start | bytes 4423680 | tf_op jit(solution)/shard_map/all_gather | solution.py:367
  8.0 147.8 %all-gather.9.cloned.1.call-start = ((), (), s32[]{:S(2)}) async-start(), calls=%async_computation.1 | async-start | bytes 1474560 | tf_op jit(solution)/shard_map/all_gather | solution.py:368
  8.8 149.6 %all-gather.11.cloned.1.call-start = ((), (), s32[]{:S(2)}) async-start(), calls=%async_computation.2 | async-start | bytes 5898240 | tf_op jit(solution)/shard_map/all_gather | solution.py:369
  9.5 167.7 %all-gather.13.cloned.1.call-start = ((), (), s32[]{:S(2)}) async-start(), calls=%async_computation.3 | async-start | bytes 5898240 | tf_op jit(solution)/shard_map/all_gather | solution.py:370
  192.6 6.0 %collective-permute-start.2 = (bf16[2,2,2,2,24,768]{5,4,3,2,1,0:T(8,128)(2,1)S(1)}, bf16[2,2,2,2,24,768]{5,4,3,2,1,0:T(8,128)(2,1)S(1)}, u32[]{:S(2)}, u32[]{:S(2)}) collective-permute-start(bf16[2,2,2,2,24,768]{5,4,3,2,1,0:T(8,128)(2,1)S(1)} %dynamic-slice_bitcast_fusion.4), channel_id=1, source_target_pairs={{0,1},{1,0},{2,3},{3,2},{4,5},{5,4},{6,7},{7,6},{8,9},{9,8},{10,11... | collective-permute-start | bytes 1769480 | tf_op jit(solution)/shard_map/ppermute | solution.py:270
  198.7 9.2 %collective-permute-start.5 = (bf16[2,2,2,24,768]{4,3,2,1,0:T(8,128)(2,1)S(1)}, bf16[2,2,2,24,768]{4,3,2,1,0:T(8,128)(2,1)S(1)}, u32[]{:S(2)}, u32[]{:S(2)}) collective-permute-start(bf16[2,2,2,24,768]{4,3,2,1,0:T(8,128)(2,1)S(1)} %dynamic-slice_bitcast_fusion.9), channel_id=1, source_target_pairs={{0,2},{1,3},{2,0},{3,1},{4,6},{5,7},{6,4},{7,5},{8,10},{9,11},{10,... | collective-permute-start | bytes 884744 | tf_op jit(solution)/shard_map/ppermute | solution.py:270
  208.1 13.3 %collective-permute-start.27 = (bf16[2,2,24,768]{3,2,1,0:T(8,128)(2,1)S(1)}, bf16[2,2,24,768]{3,2,1,0:T(8,128)(2,1)S(1)}, u32[]{:S(2)}, u32[]{:S(2)}) collective-permute-start(bf16[2,2,24,768]{3,2,1,0:T(8,128)(2,1)S(1)} %dynamic-slice_bitcast_fusion.14), channel_id=1, source_target_pairs={{0,4},{1,5},{2,6},{3,7},{4,0},{5,1},{6,2},{7,3},{8,12},{9,13},{10,... | collective-permute-start | bytes 442376 | tf_op jit(solution)/shard_map/ppermute | solution.py:270
  212.9 38.3 %collective-permute-start = (bf16[2,2,2,2,96,768]{5,4,1,2,3,0:T(8,128)(2,1)}, bf16[2,2,2,2,96,768]{5,4,1,2,3,0:T(8,128)(2,1)}, u32[]{:S(2)}, u32[]{:S(2)}) collective-permute-start(bf16[2,2,2,2,96,768]{5,4,1,2,3,0:T(8,128)(2,1)} %bitcast.275), channel_id=1, source_target_pairs={{0,1},{1,0},{2,3},{3,2},{4,5},{5,4},{6,7},{7,6},{8,9},{9,8},{10,11... | collective-permute-start | bytes 7077896 | tf_op jit(solution)/shard_map/ppermute | solution.py:270
  221.5 7.5 %collective-permute-start.28 = (bf16[2,24,768]{2,1,0:T(8,128)(2,1)S(1)}, bf16[2,24,768]{2,1,0:T(8,128)(2,1)S(1)}, u32[]{:S(2)}, u32[]{:S(2)}) collective-permute-start(bf16[2,24,768]{2,1,0:T(8,128)(2,1)S(1)} %dynamic-slice_bitcast_fusion.17), channel_id=1, source_target_pairs={{0,8},{1,9},{2,10},{3,11},{4,12},{5,13},{6,14},{7,15},{8,0},{9,1},... | collective-permute-start | bytes 221192 | tf_op jit(solution)/shard_map/ppermute | solution.py:270
  228.7 26.5 %collective-permute-start.1 = (bf16[2,2,2,2,96,768]{5,4,2,1,0,3:T(8,128)(2,1)}, bf16[2,2,2,2,96,768]{5,4,2,1,0,3:T(8,128)(2,1)}, u32[]{:S(2)}, u32[]{:S(2)}) collective-permute-start(bf16[2,2,2,2,96,768]{5,4,2,1,0,3:T(8,128)(2,1)} %bitcast.274), channel_id=1, source_target_pairs={{0,1},{1,0},{2,3},{3,2},{4,5},{5,4},{6,7},{7,6},{8,9},{9,8},{10,11... | collective-permute-start | bytes 7077896 | tf_op jit(solution)/shard_map/ppermute | solution.py:270
  229.0 11.7 %collective-permute-start.29 = (bf16[24,768]{1,0:T(8,128)(2,1)S(1)}, bf16[24,768]{1,0:T(8,128)(2,1)S(1)}, u32[]{:S(2)}, u32[]{:S(2)}) collective-permute-start(bf16[24,768]{1,0:T(8,128)(2,1)S(1)} %dynamic-slice_bitcast_fusion.20), channel_id=1, source_target_pairs={{0,16},{1,17},{2,18},{3,19},{4,20},{5,21},{6,22},{7,23},{8,24},{9,... | collective-permute-start | bytes 110600 | tf_op jit(solution)/shard_map/ppermute | solution.py:270
  240.8 5.3 collective-permute-start.30
  250.6 14.1 %collective-permute-start.32 = (bf16[2,2,24,768]{3,2,0,1:T(8,128)(2,1)S(1)}, bf16[2,2,24,768]{3,2,0,1:T(8,128)(2,1)S(1)}, u32[]{:S(2)}, u32[]{:S(2)}) collective-permute-start(bf16[2,2,24,768]{3,2,0,1:T(8,128)(2,1)S(1)} %pad_maximum_fusion.10), channel_id=1, source_target_pairs={{0,4},{1,5},{2,6},{3,7},{4,0},{5,1},{6,2},{7,3},{8,12},{9,13},{10,... | collective-permute-start | bytes 442376 | tf_op jit(solution)/shard_map/ppermute | solution.py:270
  254.7 74.1 %collective-permute-start.3 = (bf16[2,2,2,96,768]{4,3,0,1,2:T(8,128)(2,1)}, bf16[2,2,2,96,768]{4,3,0,1,2:T(8,128)(2,1)}, u32[]{:S(2)}, u32[]{:S(2)}) collective-permute-start(bf16[2,2,2,96,768]{4,3,0,1,2:T(8,128)(2,1)} %dynamic-slice_bitcast_fusion.1), channel_id=1, source_target_pairs={{0,2},{1,3},{2,0},{3,1},{4,6},{5,7},{6,4},{7,5},{8,10},{9,11},{10,... | collective-permute-start | bytes 3538952 | tf_op jit(solution)/shard_map/ppermute | solution.py:270
  260.2 72.2 %collective-permute-start.4 = (bf16[2,2,2,96,768]{4,3,2,1,0:T(8,128)(2,1)}, bf16[2,2,2,96,768]{4,3,2,1,0:T(8,128)(2,1)}, u32[]{:S(2)}, u32[]{:S(2)}) collective-permute-start(bf16[2,2,2,96,768]{4,3,2,1,0:T(8,128)(2,1)} %dynamic-slice_bitcast_fusion), channel_id=1, source_target_pairs={{0,4},{1,5},{2,6},{3,7},{4,0},{5,1},{6,2},{7,3},{8,12},{9,13},{10,... | collective-permute-start | bytes 3538952 | tf_op jit(solution)/shard_map/ppermute | solution.py:270
  395.1 11.8 %collective-permute-start.22 = (f32[4,2304]{1,0:T(4,128)}, f32[4,2304]{1,0:T(4,128)}, u32[]{:S(2)}, u32[]{:S(2)}) collective-permute-start(f32[4,2304]{1,0:T(4,128)} %concatenate.27), channel_id=1, source_target_pairs={{0,1},{1,0},{2,3},{3,2},{4,5},{5,4},{6,7},{7,6},{8,9},{9,8},{10,11... | collective-permute-start | bytes 110600 | tf_op jit(solution)/shard_map/ppermute | solution.py:270
  408.4 10.9 %collective-permute-start.23 = (f32[4,2304]{1,0:T(4,128)}, f32[4,2304]{1,0:T(4,128)}, u32[]{:S(2)}, u32[]{:S(2)}) collective-permute-start(f32[4,2304]{1,0:T(4,128)} %add.391), channel_id=1, source_target_pairs={{0,2},{1,3},{2,0},{3,1},{4,6},{5,7},{6,4},{7,5},{8,10},{9,11},{10,... | collective-permute-start | bytes 110600 | tf_op jit(solution)/shard_map/ppermute | solution.py:270
  420.1 10.6 %collective-permute-start.24 = (f32[4,2304]{1,0:T(4,128)S(1)}, f32[4,2304]{1,0:T(4,128)S(1)}, u32[]{:S(2)}, u32[]{:S(2)}) collective-permute-start(f32[4,2304]{1,0:T(4,128)S(1)} %add.392), channel_id=1, source_target_pairs={{0,4},{1,5},{2,6},{3,7},{4,0},{5,1},{6,2},{7,3},{8,12},{9,13},{10,... | collective-permute-start | bytes 110600 | tf_op jit(solution)/shard_map/ppermute | solution.py:270
  430.8 6.1 %collective-permute-start.25 = (f32[4,2304]{1,0:T(4,128)S(1)}, f32[4,2304]{1,0:T(4,128)S(1)}, u32[]{:S(2)}, u32[]{:S(2)}) collective-permute-start(f32[4,2304]{1,0:T(4,128)S(1)} %add.393), channel_id=1, source_target_pairs={{0,8},{1,9},{2,10},{3,11},{4,12},{5,13},{6,14},{7,15},{8,0},{9,1},... | collective-permute-start | bytes 110600 | tf_op jit(solution)/shard_map/ppermute | solution.py:270
  436.9 4.9 collective-permute-start.26
  439.3 18.7 %collective-permute-start.14 = (bf16[2,2,2,2,72,384]{5,4,3,2,1,0:T(8,128)(2,1)S(1)}, bf16[2,2,2,2,72,384]{5,4,3,2,1,0:T(8,128)(2,1)S(1)}, u32[]{:S(2)}, u32[]{:S(2)}) collective-permute-start(bf16[2,2,2,2,72,384]{5,4,3,2,1,0:T(8,128)(2,1)S(1)} %bitcast.294), channel_id=1, source_target_pairs={{0,1},{1,0},{2,3},{3,2},{4,5},{5,4},{6,7},{7,6},{8,9},{9,8},{10,11... | collective-permute-start | bytes 2654216 | tf_op jit(solution)/shard_map/ppermute | solution.py:270
  439.5 19.4 %collective-permute-start.6 = (bf16[2,2,2,2,72,384]{5,4,1,2,3,0:T(8,128)(2,1)S(1)}, bf16[2,2,2,2,72,384]{5,4,1,2,3,0:T(8,128)(2,1)S(1)}, u32[]{:S(2)}, u32[]{:S(2)}) collective-permute-start(bf16[2,2,2,2,72,384]{5,4,1,2,3,0:T(8,128)(2,1)S(1)} %bitcast.293), channel_id=1, source_target_pairs={{0,1},{1,0},{2,3},{3,2},{4,5},{5,4},{6,7},{7,6},{8,9},{9,8},{10,11... | collective-permute-start | bytes 2654216 | tf_op jit(solution)/shard_map/ppermute | solution.py:270
  440.1 15.3 %collective-permute-start.33 = (bf16[2,2,96,768]{3,2,1,0:T(8,128)(2,1)S(1)}, bf16[2,2,96,768]{3,2,1,0:T(8,128)(2,1)S(1)}, u32[]{:S(2)}, u32[]{:S(2)}) collective-permute-start(bf16[2,2,96,768]{3,2,1,0:T(8,128)(2,1)S(1)} %dynamic-slice_bitcast_fusion.3), channel_id=1, source_target_pairs={{0,2},{1,3},{2,0},{3,1},{4,6},{5,7},{6,4},{7,5},{8,10},{9,11},{10,... | collective-permute-start | bytes 1769480 | tf_op jit(solution)/shard_map/ppermute | solution.py:270
  440.1 16.0 %collective-permute-start.39 = (bf16[2,2,96,768]{3,2,0,1:T(8,128)(2,1)S(1)}, bf16[2,2,96,768]{3,2,0,1:T(8,128)(2,1)S(1)}, u32[]{:S(2)}, u32[]{:S(2)}) collective-permute-start(bf16[2,2,96,768]{3,2,0,1:T(8,128)(2,1)S(1)} %dynamic-slice_bitcast_fusion.2), channel_id=1, source_target_pairs={{0,4},{1,5},{2,6},{3,7},{4,0},{5,1},{6,2},{7,3},{8,12},{9,13},{10,... | collective-permute-start | bytes 1769480 | tf_op jit(solution)/shard_map/ppermute | solution.py:270
  455.6 10.0 %collective-permute-start.34 = (bf16[2,96,768]{2,1,0:T(8,128)(2,1)S(1)}, bf16[2,96,768]{2,1,0:T(8,128)(2,1)S(1)}, u32[]{:S(2)}, u32[]{:S(2)}) collective-permute-start(bf16[2,96,768]{2,1,0:T(8,128)(2,1)S(1)} %dynamic-slice_bitcast_fusion.8), channel_id=1, source_target_pairs={{0,8},{1,9},{2,10},{3,11},{4,12},{5,13},{6,14},{7,15},{8,0},{9,1},... | collective-permute-start | bytes 884744 | tf_op jit(solution)/shard_map/ppermute | solution.py:270
  456.3 16.5 %collective-permute-start.40 = (bf16[2,96,768]{2,1,0:T(8,128)(2,1)S(1)}, bf16[2,96,768]{2,1,0:T(8,128)(2,1)S(1)}, u32[]{:S(2)}, u32[]{:S(2)}) collective-permute-start(bf16[2,96,768]{2,1,0:T(8,128)(2,1)S(1)} %dynamic-slice_bitcast_fusion.7), channel_id=1, source_target_pairs={{0,8},{1,9},{2,10},{3,11},{4,12},{5,13},{6,14},{7,15},{8,0},{9,1},... | collective-permute-start | bytes 884744 | tf_op jit(solution)/shard_map/ppermute | solution.py:270
  458.2 35.4 %collective-permute-start.15 = (bf16[2,2,2,72,384]{4,3,2,1,0:T(8,128)(2,1)S(1)}, bf16[2,2,2,72,384]{4,3,2,1,0:T(8,128)(2,1)S(1)}, u32[]{:S(2)}, u32[]{:S(2)}) collective-permute-start(bf16[2,2,2,72,384]{4,3,2,1,0:T(8,128)(2,1)S(1)} %dynamic-slice_bitcast_fusion.5), channel_id=1, source_target_pairs={{0,4},{1,5},{2,6},{3,7},{4,0},{5,1},{6,2},{7,3},{8,12},{9,13},{10,... | collective-permute-start | bytes 1327112 | tf_op jit(solution)/shard_map/ppermute | solution.py:270
  459.1 35.4 %collective-permute-start.7 = (bf16[2,2,2,72,384]{4,3,0,1,2:T(8,128)(2,1)S(1)}, bf16[2,2,2,72,384]{4,3,0,1,2:T(8,128)(2,1)S(1)}, u32[]{:S(2)}, u32[]{:S(2)}) collective-permute-start(bf16[2,2,2,72,384]{4,3,0,1,2:T(8,128)(2,1)S(1)} %dynamic-slice_bitcast_fusion.6), channel_id=1, source_target_pairs={{0,2},{1,3},{2,0},{3,1},{4,6},{5,7},{6,4},{7,5},{8,10},{9,11},{10,... | collective-permute-start | bytes 1327112 | tf_op jit(solution)/shard_map/ppermute | solution.py:270
  465.7 13.9 %collective-permute-start.35 = (bf16[96,768]{1,0:T(8,128)(2,1)S(1)}, bf16[96,768]{1,0:T(8,128)(2,1)S(1)}, u32[]{:S(2)}, u32[]{:S(2)}) collective-permute-start(bf16[96,768]{1,0:T(8,128)(2,1)S(1)} %dynamic-slice_bitcast_fusion.13), channel_id=1, source_target_pairs={{0,16},{1,17},{2,18},{3,19},{4,20},{5,21},{6,22},{7,23},{8,24},{9,... | collective-permute-start | bytes 442376 | tf_op jit(solution)/shard_map/ppermute | solution.py:270
  472.9 9.9 %collective-permute-start.41 = (bf16[96,768]{1,0:T(8,128)(2,1)S(1)}, bf16[96,768]{1,0:T(8,128)(2,1)S(1)}, u32[]{:S(2)}, u32[]{:S(2)}) collective-permute-start(bf16[96,768]{1,0:T(8,128)(2,1)S(1)} %dynamic-slice_bitcast_fusion.12), channel_id=1, source_target_pairs={{0,16},{1,17},{2,18},{3,19},{4,20},{5,21},{6,22},{7,23},{8,24},{9,... | collective-permute-start | bytes 442376 | tf_op jit(solution)/shard_map/ppermute | solution.py:270
  479.6 11.7 %collective-permute-start.36 = (bf16[96,768]{1,0:T(8,128)(2,1)S(1)}, bf16[96,768]{1,0:T(8,128)(2,1)S(1)}, u32[]{:S(2)}, u32[]{:S(2)}) collective-permute-start(bf16[96,768]{1,0:T(8,128)(2,1)S(1)} %fusion.40), channel_id=1, source_target_pairs={{0,16},{1,17},{2,18},{3,19},{4,20},{5,21},{6,22},{7,23},{8,24},{9,... | collective-permute-start | bytes 442376 | tf_op jit(solution)/shard_map/ppermute | solution.py:270
  482.8 10.7 %collective-permute-start.42 = (bf16[96,768]{1,0:T(8,128)(2,1)S(1)}, bf16[96,768]{1,0:T(8,128)(2,1)S(1)}, u32[]{:S(2)}, u32[]{:S(2)}) collective-permute-start(bf16[96,768]{1,0:T(8,128)(2,1)S(1)} %fusion.39), channel_id=1, source_target_pairs={{0,16},{1,17},{2,18},{3,19},{4,20},{5,21},{6,22},{7,23},{8,24},{9,... | collective-permute-start | bytes 442376 | tf_op jit(solution)/shard_map/ppermute | solution.py:270
  491.4 10.0 %collective-permute-start.37 = (bf16[2,96,768]{2,1,0:T(8,128)(2,1)S(1)}, bf16[2,96,768]{2,1,0:T(8,128)(2,1)S(1)}, u32[]{:S(2)}, u32[]{:S(2)}) collective-permute-start(bf16[2,96,768]{2,1,0:T(8,128)(2,1)S(1)} %pad_maximum_fusion.6), channel_id=1, source_target_pairs={{0,8},{1,9},{2,10},{3,11},{4,12},{5,13},{6,14},{7,15},{8,0},{9,1},... | collective-permute-start | bytes 884744 | tf_op jit(solution)/shard_map/ppermute | solution.py:270
  493.6 12.5 %collective-permute-start.43 = (bf16[2,96,768]{2,1,0:T(8,128)(2,1)S(1)}, bf16[2,96,768]{2,1,0:T(8,128)(2,1)S(1)}, u32[]{:S(2)}, u32[]{:S(2)}) collective-permute-start(bf16[2,96,768]{2,1,0:T(8,128)(2,1)S(1)} %pad_maximum_fusion.7), channel_id=1, source_target_pairs={{0,8},{1,9},{2,10},{3,11},{4,12},{5,13},{6,14},{7,15},{8,0},{9,1},... | collective-permute-start | bytes 884744 | tf_op jit(solution)/shard_map/ppermute | solution.py:270
  493.8 12.4 %collective-permute-start.16 = (bf16[2,2,72,384]{3,2,1,0:T(8,128)(2,1)S(1)}, bf16[2,2,72,384]{3,2,1,0:T(8,128)(2,1)S(1)}, u32[]{:S(2)}, u32[]{:S(2)}) collective-permute-start(bf16[2,2,72,384]{3,2,1,0:T(8,128)(2,1)S(1)} %dynamic-slice_bitcast_fusion.10), channel_id=1, source_target_pairs={{0,2},{1,3},{2,0},{3,1},{4,6},{5,7},{6,4},{7,5},{8,10},{9,11},{10,... | collective-permute-start | bytes 663560 | tf_op jit(solution)/shard_map/ppermute | solution.py:270
  494.7 11.7 %collective-permute-start.8 = (bf16[2,2,72,384]{3,2,0,1:T(8,128)(2,1)S(1)}, bf16[2,2,72,384]{3,2,0,1:T(8,128)(2,1)S(1)}, u32[]{:S(2)}, u32[]{:S(2)}) collective-permute-start(bf16[2,2,72,384]{3,2,0,1:T(8,128)(2,1)S(1)} %dynamic-slice_bitcast_fusion.11), channel_id=1, source_target_pairs={{0,4},{1,5},{2,6},{3,7},{4,0},{5,1},{6,2},{7,3},{8,12},{9,13},{10,... | collective-permute-start | bytes 663560 | tf_op jit(solution)/shard_map/ppermute | solution.py:270
  501.5 31.6 %collective-permute-start.38 = (bf16[2,2,96,768]{3,2,0,1:T(8,128)(2,1)S(1)}, bf16[2,2,96,768]{3,2,0,1:T(8,128)(2,1)S(1)}, u32[]{:S(2)}, u32[]{:S(2)}) collective-permute-start(bf16[2,2,96,768]{3,2,0,1:T(8,128)(2,1)S(1)} %pad_maximum_fusion.4), channel_id=1, source_target_pairs={{0,4},{1,5},{2,6},{3,7},{4,0},{5,1},{6,2},{7,3},{8,12},{9,13},{10,... | collective-permute-start | bytes 1769480 | tf_op jit(solution)/shard_map/ppermute | solution.py:270
  506.1 27.1 %collective-permute-start.44 = (bf16[2,2,96,768]{3,2,0,1:T(8,128)(2,1)S(1)}, bf16[2,2,96,768]{3,2,0,1:T(8,128)(2,1)S(1)}, u32[]{:S(2)}, u32[]{:S(2)}) collective-permute-start(bf16[2,2,96,768]{3,2,0,1:T(8,128)(2,1)S(1)} %pad_maximum_fusion.5), channel_id=1, source_target_pairs={{0,4},{1,5},{2,6},{3,7},{4,0},{5,1},{6,2},{7,3},{8,12},{9,13},{10,... | collective-permute-start | bytes 1769480 | tf_op jit(solution)/shard_map/ppermute | solution.py:270
  506.3 4.8 collective-permute-start.17
  506.5 6.9 %collective-permute-start.9 = (bf16[2,72,384]{2,1,0:T(8,128)(2,1)S(1)}, bf16[2,72,384]{2,1,0:T(8,128)(2,1)S(1)}, u32[]{:S(2)}, u32[]{:S(2)}) collective-permute-start(bf16[2,72,384]{2,1,0:T(8,128)(2,1)S(1)} %dynamic-slice_bitcast_fusion.16), channel_id=1, source_target_pairs={{0,8},{1,9},{2,10},{3,11},{4,12},{5,13},{6,14},{7,15},{8,0},{9,1},... | collective-permute-start | bytes 331784 | tf_op jit(solution)/shard_map/ppermute | solution.py:270
  511.2 5.8 %collective-permute-start.18 = (bf16[72,384]{1,0:T(8,128)(2,1)S(1)}, bf16[72,384]{1,0:T(8,128)(2,1)S(1)}, u32[]{:S(2)}, u32[]{:S(2)}) collective-permute-start(bf16[72,384]{1,0:T(8,128)(2,1)S(1)} %dynamic-slice_bitcast_fusion.18), channel_id=1, source_target_pairs={{0,16},{1,17},{2,18},{3,19},{4,20},{5,21},{6,22},{7,23},{8,24},{9,... | collective-permute-start | bytes 165896 | tf_op jit(solution)/shard_map/ppermute | solution.py:270
  513.4 6.9 %collective-permute-start.10 = (bf16[72,384]{1,0:T(8,128)(2,1)S(1)}, bf16[72,384]{1,0:T(8,128)(2,1)S(1)}, u32[]{:S(2)}, u32[]{:S(2)}) collective-permute-start(bf16[72,384]{1,0:T(8,128)(2,1)S(1)} %dynamic-slice_bitcast_fusion.19), channel_id=1, source_target_pairs={{0,16},{1,17},{2,18},{3,19},{4,20},{5,21},{6,22},{7,23},{8,24},{9,... | collective-permute-start | bytes 165896 | tf_op jit(solution)/shard_map/ppermute | solution.py:270
  517.0 5.2 collective-permute-start.19
  520.4 5.2 collective-permute-start.11
  522.3 6.0 %collective-permute-start.20 = (bf16[2,72,384]{2,1,0:T(8,128)(2,1)S(1)}, bf16[2,72,384]{2,1,0:T(8,128)(2,1)S(1)}, u32[]{:S(2)}, u32[]{:S(2)}) collective-permute-start(bf16[2,72,384]{2,1,0:T(8,128)(2,1)S(1)} %pad_maximum_fusion.12), channel_id=1, source_target_pairs={{0,8},{1,9},{2,10},{3,11},{4,12},{5,13},{6,14},{7,15},{8,0},{9,1},... | collective-permute-start | bytes 331784 | tf_op jit(solution)/shard_map/ppermute | solution.py:270
  525.6 5.2 collective-permute-start.12
  529.1 8.0 %collective-permute-start.21 = (bf16[2,2,72,384]{3,2,0,1:T(8,128)(2,1)}, bf16[2,2,72,384]{3,2,0,1:T(8,128)(2,1)}, u32[]{:S(2)}, u32[]{:S(2)}) collective-permute-start(bf16[2,2,72,384]{3,2,0,1:T(8,128)(2,1)} %pad_maximum_fusion.9), channel_id=1, source_target_pairs={{0,4},{1,5},{2,6},{3,7},{4,0},{5,1},{6,2},{7,3},{8,12},{9,13},{10,... | collective-permute-start | bytes 663560 | tf_op jit(solution)/shard_map/ppermute | solution.py:270
  531.6 6.7 %collective-permute-start.13 = (bf16[2,2,72,384]{3,2,0,1:T(8,128)(2,1)}, bf16[2,2,72,384]{3,2,0,1:T(8,128)(2,1)}, u32[]{:S(2)}, u32[]{:S(2)}) collective-permute-start(bf16[2,2,72,384]{3,2,0,1:T(8,128)(2,1)} %pad_maximum_fusion.8), channel_id=1, source_target_pairs={{0,4},{1,5},{2,6},{3,7},{4,0},{5,1},{6,2},{7,3},{8,12},{9,13},{10,... | collective-permute-start | bytes 663560 | tf_op jit(solution)/shard_map/ppermute | solution.py:270
  (64 other events, 475.1 us)
Sparse Core Ops, SparseCore 0:
  9.7 33.4 all-gather.6
  44.7 41.9 all-gather.8
  88.3 41.5 all-gather.10
  131.2 45.9 all-gather.12
